TPU v7x, 256 devices: a whole 4x4x8 slice. The times are simulated.
256 devices in a mesh: seq: 32 (over y, x, core), head: 8 (over z).
Axes of the slice: x: 4, y: 4, z: 8, core: 2. Of those that a mesh axis runs over, the one named last changes fastest.
Arguments:
- tokens: bfloat16 [4096, 4096], P('seq'), may hold values from -6 to 6
- key_weight: bfloat16 [4096, 4096], P(None, 'head'), may hold values from -0.09375 to 0.09375
- queries: bfloat16 [4096, 4096], P('seq', 'head'), may hold values from -6 to 6
- values: bfloat16 [4096, 4096], P('seq', 'head'), may hold values from -6 to 6
- grad_out: bfloat16 [4096, 4096], P('seq', 'head'), may hold values from -6 to 6
- inner_start: float32 [32, 128, 128], P('head'), may hold values from -0.5 to 0.5
- head_rate: float32 [32], P('head'), may hold values from 0.01 to 1
Outputs:
- grad_tokens: bfloat16 [4096, 4096], P('seq', 'head')
- grad_key_weight: float32 [4096, 4096], P('seq', 'head')
- grad_query: bfloat16 [4096, 4096], P('seq', 'head')
- grad_value: bfloat16 [4096, 4096], P('seq', 'head')
All inputs are finite; a program needn't handle non-finite values.
Results may differ from a plain program's by a relative error of at most 0.029.
Values may be sent and summed in bfloat16 or wider, within the bound.
A program may use at most 128 MiB of HBM per device.

v0:
```python
import jax
import jax.numpy as jnp
from jax import lax
from jax.sharding import PartitionSpec as P

MINI = 16


rate_base = 0.1
norm_eps = 1e-06
best = lax.Precision.HIGHEST


def from_behind(block, axis, distance):
    devices = range(lax.axis_size(axis))
    route = [(i - distance, i) for i in devices if i - distance in devices]
    return lax.ppermute(block, axis, route)


def matmul_heads(left, right):
    return jnp.einsum("hij,hjk->hik", left, right, precision=best)


def project(keys_b, state):
    return jnp.einsum("bhi,hij->bhj", keys_b, state, precision=best)


def outer(keys_b, other):
    return jnp.einsum("bhi,bhj->hij", keys_b, other, precision=best)


def per_device(tokens, key_weight, queries, values, grad_out, inner_start, head_rate):
    tok_rows, model_width = tokens.shape
    local_heads, width = (inner_start.shape[0], inner_start.shape[1])
    batches = tok_rows // MINI
    shape4 = (batches, MINI, local_heads, width)
    keys_raw = jnp.dot(tokens, key_weight, preferred_element_type=jnp.float32).reshape(shape4)
    inv_norm = lax.rsqrt(jnp.sum(keys_raw * keys_raw, axis=-1, keepdims=True) + norm_eps)
    keys = keys_raw * inv_norm
    value_rows = values.astype(jnp.float32).reshape(shape4)
    query_rows = queries.astype(jnp.float32).reshape(shape4)
    grad_rows = grad_out.astype(jnp.float32).reshape(shape4)
    rate = (rate_base * head_rate)[:, None, None]
    rate_rows = (rate_base * head_rate)[None, :, None]
    ident = jnp.broadcast_to(jnp.eye(width, dtype=jnp.float32), (local_heads, width, width))
    zeros = jnp.zeros_like(inner_start)

    def local_maps(carry, batch):
        keys_b, value_b = batch
        linear, offset = carry
        linear = linear - rate * outer(keys_b, project(keys_b, linear))
        offset = offset - rate * outer(keys_b, project(keys_b, offset) - value_b)
        return ((linear, offset), None)

    (linear, offset), _ = lax.scan(local_maps, (ident, zeros), (keys, value_rows))
    products = jnp.einsum("tbhi,tbhj->thij", query_rows, grad_rows, precision=best)

    def adjoint_sum(acc, batch):
        keys_b, product = batch
        total = acc + product
        return (total - rate * outer(keys_b, project(keys_b, total)), None)

    carried, _ = lax.scan(adjoint_sum, zeros, (keys, products), reverse=True)
    turned = jnp.swapaxes(linear, 1, 2)
    index = lax.axis_index("seq")
    count = lax.axis_size("seq")

    def relay(step, state):
        passed = from_behind(
            (matmul_heads(linear, state) + offset).astype(jnp.bfloat16), "seq", 1
        ).astype(jnp.float32)
        return jnp.where(index == 0, inner_start, passed)

    start = lax.fori_loop(0, count - 1, relay, inner_start)

    def relay_back(step, state):
        return from_behind(
            (matmul_heads(turned, state) + carried).astype(jnp.bfloat16), "seq", -1
        ).astype(jnp.float32)

    incoming = lax.fori_loop(0, count - 1, relay_back, zeros)

    def sweep(state, batch):
        keys_b, value_b = batch
        new = state - rate * outer(keys_b, project(keys_b, state) - value_b)
        return (new, (state, new))

    _, (before, after) = lax.scan(sweep, start, (keys, value_rows))
    grad_query = jnp.einsum("tbhj,thij->tbhi", grad_rows, after, precision=best)
    grad_query = grad_query.reshape(tok_rows, local_heads * width).astype(jnp.bfloat16)

    def descend(carry, batch):
        keys_b, value_b, product, state = batch
        adjoint = carry + product
        resid = project(keys_b, state) - value_b
        keyed = project(keys_b, adjoint)
        key_step = -rate_rows * (
            jnp.einsum("bhj,hij->bhi", resid, adjoint, precision=best)
            + jnp.einsum("bhj,hij->bhi", keyed, state, precision=best)
        )
        return (adjoint - rate * outer(keys_b, keyed), (key_step, rate_rows * keyed))

    _, (key_adj, grad_value) = lax.scan(
        descend, incoming, (keys, value_rows, products, before), reverse=True
    )
    grad_value = grad_value.reshape(tok_rows, local_heads * width).astype(jnp.bfloat16)
    along = jnp.sum(keys * key_adj, axis=-1, keepdims=True)
    raw_adj = (
        ((key_adj - keys * along) * inv_norm)
        .astype(jnp.bfloat16)
        .reshape(tok_rows, local_heads * width)
    )
    grad_key_weight = lax.psum_scatter(
        lax.dot_general(
            tokens, raw_adj, (((0,), (0,)), ((), ())), preferred_element_type=jnp.float32
        ).astype(jnp.bfloat16),
        "seq",
        scatter_dimension=0,
        tiled=True,
    ).astype(jnp.float32)
    partial_sum = lax.dot_general(
        raw_adj, key_weight, (((1,), (1,)), ((), ())), preferred_element_type=jnp.float32
    )
    grad_tokens = lax.psum_scatter(
        partial_sum.astype(jnp.bfloat16), "head", scatter_dimension=1, tiled=True
    )
    return (grad_tokens, grad_key_weight, grad_query, grad_value)


def solution(mesh):
    placed = (
        P("seq", None),
        P(None, "head"),
        P("seq", "head"),
        P("seq", "head"),
        P("seq", "head"),
        P("head", None, None),
        P("head"),
    )
    return jax.shard_map(
        per_device,
        mesh=mesh,
        in_specs=placed,
        out_specs=(P("seq", "head"), P("seq", "head"), P("seq", "head"), P("seq", "head")),
        check_vma=False,
    )
```

profile of v0, /device:TPU:1, one launch (start us, length us, event | category | flops | bytes accessed | tf_op | source)
XLA Modules:
  0.0 830.8 jit_solution(1822055576168160369)
XLA Ops:
  12.6 15.6 %while.86 = (s32[]{:T(128)}, f32[4,128,128]{2,1,0:T(8,128)S(1)}, f32[4,128,128]{2,1,0:T(8,128)S(1)}, f32[4,1,1]{0,2,1:T(1,128)S(1)}, f32[8,16,4,128]{3,1,2,0:T(8...) while((s32[]{:T(128)}, f32[4,128,128]{2,1,0:T(8,128)S(1)}, ...), condition=%wide.region_2.3_spmd.clone, body=%wide.region_1.2_spmd.clone.sunk | while | flops 50733056 | bytes 1869932 | solution.py:55
  29.1 246.5 %while.83 = (s32[]{:T(128)}, f32[4,128,128]{2,1,0:T(8,128)S(1)}, pred[]{:T(512)}, f32[4,128,128]{2,1,0:T(8,128)S(1)}, f32[4,128,128]{2,1,0:T(8,128)S(1)}, /*index=5*/f32[4,128,128]{2,1,0:T(8,128)S(1)}, s32[]{:T(128)}) while((s32[]{:T(128)}, f32[4,128,128]{2,1,0:T(8,128)S(1)}, pred[]{:T(512)}, f32[4,128,128]{2,1,0:T(8,128)S(1)}, ...), condition=%wide.region_8.9_spmd, body=%wide.region_7.8_spmd.sunk | while | flops 100925440 | bytes 2097270 | solution.py:74
  275.6 25.2 %while.84 = (s32[]{:T(128)}, f32[4,128,128]{2,1,0:T(8,128)S(1)}, f32[8,4,128,128]{3,2,1,0:T(8,128)}, f32[8,4,128,128]{3,2,1,0:T(8,128)}, f32[4,1,1]{0,2,1:T(1,12...) while((s32[]{:T(128)}, f32[4,128,128]{2,1,0:T(8,128)S(1)}, ...), condition=%wide.region_10.11_spmd, body=%wide.region_9.10_spmd.sunk | while | flops 25305088 | bytes 1739861 | solution.py:88
  302.6 23.1 %while.87 = (s32[]{:T(128)}, f32[4,128,128]{2,1,0:T(8,128)S(1)}, f32[8,4,128,128]{3,2,1,0:T(8,128)}, f32[4,1,1]{0,2,1:T(1,128)S(1)}, f32[8,16,4,128]{3,1,2,0:T(8,128)S(1)}, /*index=5*/s32[]{:T(128)}, s32[]{:T(128)}, s32[]{:T(128)}) while((s32[]{:T(128)}, f32[4,128,128]{2,1,0:T(8,128)S(1)}, f32[8,4,128,128]{3,2,1,0:T(8,128)}, ...), condition=%wide.region_4.5_spmd.clone, body=%wide.region_3.4_spmd.clone.sunk | while | flops 25559044 | bytes 1445482 | solution.py:63
  325.7 276.4 %while.88 = (s32[]{:T(128)}, f32[4,128,128]{2,1,0:T(8,128)S(1)}, f32[4,128,128]{2,1,0:T(8,128)S(1)}, f32[4,128,128]{2,1,0:T(8,128)S(1)}, s32[]{:T(128)}, /*index=5*/s32[]{:T(128)}) while((s32[]{:T(128)}, f32[4,128,128]{2,1,0:T(8,128)S(1)}, f32[4,128,128]{2,1,0:T(8,128)S(1)}, f32[4,128,128]{2,1,0:T(8,128)S(1)}, s32[]{:T(128)}, ...), condition=%wide.region_6.7_spmd.clone, body=%wide.region_5.6_spmd.clone.sunk | while | flops 100925440 | bytes 1835127 | solution.py:81
  328.1 7.2 collective-permute-done.1
  346.3 7.2 collective-permute-done.1
  364.6 7.2 collective-permute-done.1
  382.8 7.2 collective-permute-done.1
  392.4 6.5 collective-permute-done.1
  401.2 6.5 collective-permute-done.1
  410.1 6.5 collective-permute-done.1
  418.9 6.5 collective-permute-done.1
  436.6 6.5 collective-permute-done.1
  445.4 6.5 collective-permute-done.1
  463.1 6.5 collective-permute-done.1
  507.3 6.5 collective-permute-done.1
  533.8 6.5 collective-permute-done.1
  542.6 6.5 collective-permute-done.1
  551.5 6.5 collective-permute-done.1
  595.6 6.5 collective-permute-done.1
  602.2 57.4 %while.85 = (s32[]{:T(128)}, f32[4,128,128]{2,1,0:T(8,128)S(1)}, f32[8,16,4,128]{3,1,2,0:T(8,128)S(1)}, bf16[8,16,4,128]{3,1,2,0:T(8,128)(2,1)S(1)}, f32[8,4,128...) while((s32[]{:T(128)}, f32[4,128,128]{2,1,0:T(8,128)S(1)}, ...), condition=%wide.region_12.13_spmd, body=%wide.region_11.12_spmd.sunk | while | flops 63275008 | bytes 2792077 | solution.py:103
  680.9 105.0 %reduce-scatter.7.cloned.1.call-done = bf16[128,512]{1,0:T(8,128)(2,1)} async-done(((bf16[4096,512]{1,0:T(8,128)(2,1)}), bf16[128,512]{1,0:T(8,128)(2,1)}) %reduce-scatter.7.cloned.1.call-update) | async-done | bytes 131088
  787.7 36.2 %reduce-scatter.5.cloned.1.call-done = bf16[128,512]{1,0:T(8,128)(2,1)} async-done(((bf16[128,4096]{1,0:T(8,128)(2,1)}), bf16[128,512]{1,0:T(8,128)(2,1)}) %reduce-scatter.5.cloned.1.call-update) | async-done | bytes 131088 | tf_op jit(solution)/shard_map/reduce_scatter | solution.py:124
  (405 shorter events, 565.9 us)
Async XLA Ops:
  7.2 778.7 %reduce-scatter.7.cloned.1.call-start = ((), (), s32[]{:S(2)}) async-start(), calls=%async_computation.3 | async-start | bytes 4325376
  125.6 8.4 %collective-permute-start = (bf16[4,128,128]{2,1,0:T(8,128)(2,1)S(1)}, bf16[4,128,128]{2,1,0:T(8,128)(2,1)S(1)}, u32[]{:S(2)}, u32[]{:S(2)}) collective-permute-start(bf16[4,128,128]{2,1,0:T(8,128)(2,1)S(1)} %fusion.136), channel_id=1, source_target_pairs={{0,8},{8,16},{16,24},{24,32},{32,40},{40,48},{48,56},{56,64},{64,7... | collective-permute-start | bytes 393224 | tf_op jit(solution)/shard_map/while/body/eval_jaxpr/ppermute | solution.py:17
  134.5 8.4 %collective-permute-start = (bf16[4,128,128]{2,1,0:T(8,128)(2,1)S(1)}, bf16[4,128,128]{2,1,0:T(8,128)(2,1)S(1)}, u32[]{:S(2)}, u32[]{:S(2)}) collective-permute-start(bf16[4,128,128]{2,1,0:T(8,128)(2,1)S(1)} %fusion.136), channel_id=1, source_target_pairs={{0,8},{8,16},{16,24},{24,32},{32,40},{40,48},{48,56},{56,64},{64,7... | collective-permute-start | bytes 393224 | tf_op jit(solution)/shard_map/while/body/eval_jaxpr/ppermute | solution.py:17
  143.3 8.4 %collective-permute-start = (bf16[4,128,128]{2,1,0:T(8,128)(2,1)S(1)}, bf16[4,128,128]{2,1,0:T(8,128)(2,1)S(1)}, u32[]{:S(2)}, u32[]{:S(2)}) collective-permute-start(bf16[4,128,128]{2,1,0:T(8,128)(2,1)S(1)} %fusion.136), channel_id=1, source_target_pairs={{0,8},{8,16},{16,24},{24,32},{32,40},{40,48},{48,56},{56,64},{64,7... | collective-permute-start | bytes 393224 | tf_op jit(solution)/shard_map/while/body/eval_jaxpr/ppermute | solution.py:17
  152.2 8.4 %collective-permute-start = (bf16[4,128,128]{2,1,0:T(8,128)(2,1)S(1)}, bf16[4,128,128]{2,1,0:T(8,128)(2,1)S(1)}, u32[]{:S(2)}, u32[]{:S(2)}) collective-permute-start(bf16[4,128,128]{2,1,0:T(8,128)(2,1)S(1)} %fusion.136), channel_id=1, source_target_pairs={{0,8},{8,16},{16,24},{24,32},{32,40},{40,48},{48,56},{56,64},{64,7... | collective-permute-start | bytes 393224 | tf_op jit(solution)/shard_map/while/body/eval_jaxpr/ppermute | solution.py:17
  161.0 8.4 %collective-permute-start = (bf16[4,128,128]{2,1,0:T(8,128)(2,1)S(1)}, bf16[4,128,128]{2,1,0:T(8,128)(2,1)S(1)}, u32[]{:S(2)}, u32[]{:S(2)}) collective-permute-start(bf16[4,128,128]{2,1,0:T(8,128)(2,1)S(1)} %fusion.136), channel_id=1, source_target_pairs={{0,8},{8,16},{16,24},{24,32},{32,40},{40,48},{48,56},{56,64},{64,7... | collective-permute-start | bytes 393224 | tf_op jit(solution)/shard_map/while/body/eval_jaxpr/ppermute | solution.py:17
  169.8 8.4 %collective-permute-start = (bf16[4,128,128]{2,1,0:T(8,128)(2,1)S(1)}, bf16[4,128,128]{2,1,0:T(8,128)(2,1)S(1)}, u32[]{:S(2)}, u32[]{:S(2)}) collective-permute-start(bf16[4,128,128]{2,1,0:T(8,128)(2,1)S(1)} %fusion.136), channel_id=1, source_target_pairs={{0,8},{8,16},{16,24},{24,32},{32,40},{40,48},{48,56},{56,64},{64,7... | collective-permute-start | bytes 393224 | tf_op jit(solution)/shard_map/while/body/eval_jaxpr/ppermute | solution.py:17
  178.7 8.4 %collective-permute-start = (bf16[4,128,128]{2,1,0:T(8,128)(2,1)S(1)}, bf16[4,128,128]{2,1,0:T(8,128)(2,1)S(1)}, u32[]{:S(2)}, u32[]{:S(2)}) collective-permute-start(bf16[4,128,128]{2,1,0:T(8,128)(2,1)S(1)} %fusion.136), channel_id=1, source_target_pairs={{0,8},{8,16},{16,24},{24,32},{32,40},{40,48},{48,56},{56,64},{64,7... | collective-permute-start | bytes 393224 | tf_op jit(solution)/shard_map/while/body/eval_jaxpr/ppermute | solution.py:17
  187.5 8.4 %collective-permute-start = (bf16[4,128,128]{2,1,0:T(8,128)(2,1)S(1)}, bf16[4,128,128]{2,1,0:T(8,128)(2,1)S(1)}, u32[]{:S(2)}, u32[]{:S(2)}) collective-permute-start(bf16[4,128,128]{2,1,0:T(8,128)(2,1)S(1)} %fusion.136), channel_id=1, source_target_pairs={{0,8},{8,16},{16,24},{24,32},{32,40},{40,48},{48,56},{56,64},{64,7... | collective-permute-start | bytes 393224 | tf_op jit(solution)/shard_map/while/body/eval_jaxpr/ppermute | solution.py:17
  196.4 8.4 %collective-permute-start = (bf16[4,128,128]{2,1,0:T(8,128)(2,1)S(1)}, bf16[4,128,128]{2,1,0:T(8,128)(2,1)S(1)}, u32[]{:S(2)}, u32[]{:S(2)}) collective-permute-start(bf16[4,128,128]{2,1,0:T(8,128)(2,1)S(1)} %fusion.136), channel_id=1, source_target_pairs={{0,8},{8,16},{16,24},{24,32},{32,40},{40,48},{48,56},{56,64},{64,7... | collective-permute-start | bytes 393224 | tf_op jit(solution)/shard_map/while/body/eval_jaxpr/ppermute | solution.py:17
  205.2 8.4 %collective-permute-start = (bf16[4,128,128]{2,1,0:T(8,128)(2,1)S(1)}, bf16[4,128,128]{2,1,0:T(8,128)(2,1)S(1)}, u32[]{:S(2)}, u32[]{:S(2)}) collective-permute-start(bf16[4,128,128]{2,1,0:T(8,128)(2,1)S(1)} %fusion.136), channel_id=1, source_target_pairs={{0,8},{8,16},{16,24},{24,32},{32,40},{40,48},{48,56},{56,64},{64,7... | collective-permute-start | bytes 393224 | tf_op jit(solution)/shard_map/while/body/eval_jaxpr/ppermute | solution.py:17
  214.0 8.4 %collective-permute-start = (bf16[4,128,128]{2,1,0:T(8,128)(2,1)S(1)}, bf16[4,128,128]{2,1,0:T(8,128)(2,1)S(1)}, u32[]{:S(2)}, u32[]{:S(2)}) collective-permute-start(bf16[4,128,128]{2,1,0:T(8,128)(2,1)S(1)} %fusion.136), channel_id=1, source_target_pairs={{0,8},{8,16},{16,24},{24,32},{32,40},{40,48},{48,56},{56,64},{64,7... | collective-permute-start | bytes 393224 | tf_op jit(solution)/shard_map/while/body/eval_jaxpr/ppermute | solution.py:17
  222.9 8.4 %collective-permute-start = (bf16[4,128,128]{2,1,0:T(8,128)(2,1)S(1)}, bf16[4,128,128]{2,1,0:T(8,128)(2,1)S(1)}, u32[]{:S(2)}, u32[]{:S(2)}) collective-permute-start(bf16[4,128,128]{2,1,0:T(8,128)(2,1)S(1)} %fusion.136), channel_id=1, source_target_pairs={{0,8},{8,16},{16,24},{24,32},{32,40},{40,48},{48,56},{56,64},{64,7... | collective-permute-start | bytes 393224 | tf_op jit(solution)/shard_map/while/body/eval_jaxpr/ppermute | solution.py:17
  231.7 8.4 %collective-permute-start = (bf16[4,128,128]{2,1,0:T(8,128)(2,1)S(1)}, bf16[4,128,128]{2,1,0:T(8,128)(2,1)S(1)}, u32[]{:S(2)}, u32[]{:S(2)}) collective-permute-start(bf16[4,128,128]{2,1,0:T(8,128)(2,1)S(1)} %fusion.136), channel_id=1, source_target_pairs={{0,8},{8,16},{16,24},{24,32},{32,40},{40,48},{48,56},{56,64},{64,7... | collective-permute-start | bytes 393224 | tf_op jit(solution)/shard_map/while/body/eval_jaxpr/ppermute | solution.py:17
  326.2 9.1 %collective-permute-start.1 = (bf16[4,128,128]{2,1,0:T(8,128)(2,1)S(1)}, bf16[4,128,128]{2,1,0:T(8,128)(2,1)S(1)}, u32[]{:S(2)}, u32[]{:S(2)}) collective-permute-start(bf16[4,128,128]{2,1,0:T(8,128)(2,1)S(1)} %fusion.169), channel_id=1, source_target_pairs={{8,0},{16,8},{24,16},{32,24},{40,32},{48,40},{56,48},{64,56},{72,6... | collective-permute-start | bytes 393224 | tf_op jit(solution)/shard_map/while/body/eval_jaxpr/ppermute | solution.py:17
  344.4 9.1 %collective-permute-start.1 = (bf16[4,128,128]{2,1,0:T(8,128)(2,1)S(1)}, bf16[4,128,128]{2,1,0:T(8,128)(2,1)S(1)}, u32[]{:S(2)}, u32[]{:S(2)}) collective-permute-start(bf16[4,128,128]{2,1,0:T(8,128)(2,1)S(1)} %fusion.169), channel_id=1, source_target_pairs={{8,0},{16,8},{24,16},{32,24},{40,32},{48,40},{56,48},{64,56},{72,6... | collective-permute-start | bytes 393224 | tf_op jit(solution)/shard_map/while/body/eval_jaxpr/ppermute | solution.py:17
  362.7 9.1 %collective-permute-start.1 = (bf16[4,128,128]{2,1,0:T(8,128)(2,1)S(1)}, bf16[4,128,128]{2,1,0:T(8,128)(2,1)S(1)}, u32[]{:S(2)}, u32[]{:S(2)}) collective-permute-start(bf16[4,128,128]{2,1,0:T(8,128)(2,1)S(1)} %fusion.169), channel_id=1, source_target_pairs={{8,0},{16,8},{24,16},{32,24},{40,32},{48,40},{56,48},{64,56},{72,6... | collective-permute-start | bytes 393224 | tf_op jit(solution)/shard_map/while/body/eval_jaxpr/ppermute | solution.py:17
  380.9 9.1 %collective-permute-start.1 = (bf16[4,128,128]{2,1,0:T(8,128)(2,1)S(1)}, bf16[4,128,128]{2,1,0:T(8,128)(2,1)S(1)}, u32[]{:S(2)}, u32[]{:S(2)}) collective-permute-start(bf16[4,128,128]{2,1,0:T(8,128)(2,1)S(1)} %fusion.169), channel_id=1, source_target_pairs={{8,0},{16,8},{24,16},{32,24},{40,32},{48,40},{56,48},{64,56},{72,6... | collective-permute-start | bytes 393224 | tf_op jit(solution)/shard_map/while/body/eval_jaxpr/ppermute | solution.py:17
  417.0 8.4 %collective-permute-start.1 = (bf16[4,128,128]{2,1,0:T(8,128)(2,1)S(1)}, bf16[4,128,128]{2,1,0:T(8,128)(2,1)S(1)}, u32[]{:S(2)}, u32[]{:S(2)}) collective-permute-start(bf16[4,128,128]{2,1,0:T(8,128)(2,1)S(1)} %fusion.169), channel_id=1, source_target_pairs={{8,0},{16,8},{24,16},{32,24},{40,32},{48,40},{56,48},{64,56},{72,6... | collective-permute-start | bytes 393224 | tf_op jit(solution)/shard_map/while/body/eval_jaxpr/ppermute | solution.py:17
  461.2 8.4 %collective-permute-start.1 = (bf16[4,128,128]{2,1,0:T(8,128)(2,1)S(1)}, bf16[4,128,128]{2,1,0:T(8,128)(2,1)S(1)}, u32[]{:S(2)}, u32[]{:S(2)}) collective-permute-start(bf16[4,128,128]{2,1,0:T(8,128)(2,1)S(1)} %fusion.169), channel_id=1, source_target_pairs={{8,0},{16,8},{24,16},{32,24},{40,32},{48,40},{56,48},{64,56},{72,6... | collective-permute-start | bytes 393224 | tf_op jit(solution)/shard_map/while/body/eval_jaxpr/ppermute | solution.py:17
  505.3 8.4 %collective-permute-start.1 = (bf16[4,128,128]{2,1,0:T(8,128)(2,1)S(1)}, bf16[4,128,128]{2,1,0:T(8,128)(2,1)S(1)}, u32[]{:S(2)}, u32[]{:S(2)}) collective-permute-start(bf16[4,128,128]{2,1,0:T(8,128)(2,1)S(1)} %fusion.169), channel_id=1, source_target_pairs={{8,0},{16,8},{24,16},{32,24},{40,32},{48,40},{56,48},{64,56},{72,6... | collective-permute-start | bytes 393224 | tf_op jit(solution)/shard_map/while/body/eval_jaxpr/ppermute | solution.py:17
  549.5 8.4 %collective-permute-start.1 = (bf16[4,128,128]{2,1,0:T(8,128)(2,1)S(1)}, bf16[4,128,128]{2,1,0:T(8,128)(2,1)S(1)}, u32[]{:S(2)}, u32[]{:S(2)}) collective-permute-start(bf16[4,128,128]{2,1,0:T(8,128)(2,1)S(1)} %fusion.169), channel_id=1, source_target_pairs={{8,0},{16,8},{24,16},{32,24},{40,32},{48,40},{56,48},{64,56},{72,6... | collective-permute-start | bytes 393224 | tf_op jit(solution)/shard_map/while/body/eval_jaxpr/ppermute | solution.py:17
  593.7 8.4 %collective-permute-start.1 = (bf16[4,128,128]{2,1,0:T(8,128)(2,1)S(1)}, bf16[4,128,128]{2,1,0:T(8,128)(2,1)S(1)}, u32[]{:S(2)}, u32[]{:S(2)}) collective-permute-start(bf16[4,128,128]{2,1,0:T(8,128)(2,1)S(1)} %fusion.169), channel_id=1, source_target_pairs={{8,0},{16,8},{24,16},{32,24},{40,32},{48,40},{56,48},{64,56},{72,6... | collective-permute-start | bytes 393224 | tf_op jit(solution)/shard_map/while/body/eval_jaxpr/ppermute | solution.py:17
  672.0 152.0 %reduce-scatter.5.cloned.1.call-start = ((), (), s32[]{:S(2)}) async-start(), calls=%async_computation.2 | async-start | bytes 1179648 | tf_op jit(solution)/shard_map/reduce_scatter | solution.py:124
  (51 other events, 501.3 us)
Sparse Core Ops, SparseCore 0:
  672.1 113.7 reduce-scatter.6
  789.1 34.7 reduce-scatter.4
where the time goes:
time: 839 us; the launch traced here: 831 us
  waiting for transfers between devices  404 us (48%)
  starting transfers between devices  232 us (28%)
  matrix products  155 us (18%)
  local copies, waits for them, and re-layouts  17.9 us (2%)
  between operations  14.4 us (2%)
    ppermute x62, waiting for transfers between devices, from_behind(): return lax.ppermute(block, axis, route)  263 us
    ppermute x62, starting transfers between devices, from_behind(): return lax.ppermute(block, axis, route)  232 us
    unnamed x3, waiting for transfers between devices  105 us
    dot_general x40, matrix products, outer(): return jnp.einsum('bhi,bhj->hij', keys_b, other, precision=best)  45.9 us
    dot_general x48, matrix products, project(): return jnp.einsum('bhi,hij->bhj', keys_b, state, precision=best)  45.4 us
    reduce_scatter x1, waiting for transfers between devices, per_device(): lax.psum_scatter(partial_sum.astype(jnp.bfloat16), 'head', scatter_dimens...  36.2 us
    dot_general x62, matrix products, matmul_heads(): return jnp.einsum('hij,hjk->hik', left, right, precision=best)  24.4 us
  transfers between devices with their start and end apart: 64, of which 64 were waited for; matrix products, arithmetic and copies ran while one was open for 1% of the time, Pallas kernels for 0%

commit v1 on v0

v1 whole, which is shorter than its diff:
```python
import jax
import jax.numpy as jnp
from jax import lax
from jax.experimental import pallas as pl
from jax.experimental.pallas import tpu as pltpu
from jax.sharding import PartitionSpec as P

MESH = pl.DeviceIdType.MESH
bf16 = jnp.bfloat16
f32 = jnp.float32
rate_base = 0.1
norm_eps = 1e-06
W = 128
NH = 4
NX, NY, NC = 4, 4, 2
ROW = NX * NC
NS = ROW * NY
NZ = 8


def mm(a, b):
    return lax.dot_general(a, b, (((1,), (0,)), ((), ())), preferred_element_type=f32)


def nt(a, b):
    return lax.dot_general(a, b, (((1,), (1,)), ((), ())), preferred_element_type=f32)


def tn(a, b):
    return lax.dot_general(a, b, (((0,), (0,)), ((), ())), preferred_element_type=f32)


def batch_of():
    rows = lax.broadcasted_iota(jnp.int32, (W, W), 0) >> 4
    cols = lax.broadcasted_iota(jnp.int32, (W, W), 1) >> 4
    return rows, cols


def local_maps(kraw, v, q, g, r):
    bi, bj = batch_of()
    inv = lax.rsqrt(jnp.sum(kraw * kraw, axis=1, keepdims=True) + norm_eps)
    k = kraw * inv
    kb = k.astype(bf16)
    m = r * nt(kb, kb)
    x1 = jnp.where(((bi >> 1) == (bj >> 1)) & (bi > bj), m, 0.0)
    x2 = jnp.where(((bi >> 2) == (bj >> 2)) & ((bi >> 1) > (bj >> 1)), m, 0.0)
    x3 = jnp.where((bi >> 2) > (bj >> 2), m, 0.0)
    rows = lax.broadcasted_iota(jnp.int32, (W, W), 0)
    cols = lax.broadcasted_iota(jnp.int32, (W, W), 1)
    t1 = jnp.where(rows == cols, 1.0, 0.0) - x1
    t1b = t1.astype(bf16)
    t2 = t1 - mm(mm(t1b, x2.astype(bf16)).astype(bf16), t1b)
    t2b = t2.astype(bf16)
    t3 = t2 - mm(mm(t2b, x3.astype(bf16)).astype(bf16), t2b)
    tb = t3.astype(bf16)
    tk = mm(tb, kb).astype(bf16)
    tv = mm(tb, v)
    z = mm(jnp.where(bi <= bj, nt(kb, q), 0.0).astype(bf16), g).astype(bf16)
    ttk = tn(tb, kb).astype(bf16)
    ttz = tn(tb, z)
    e0 = (-r * tn(tk, kb)).astype(bf16)
    f0 = (r * tn(tv.astype(bf16), kb)).astype(bf16)
    e1 = (-r * tn(kb, tk)).astype(bf16)
    f1 = (tn(g, q) - r * tn(ttz.astype(bf16), kb)).astype(bf16)
    return k, inv, kb, tk, tv, ttk, ttz, e0, f0, e1, f1


def join(a, b):
    return a.astype(f32) + b.astype(f32) + mm(a.astype(bf16), b[:W].astype(bf16))


def apply(state, m):
    return state + mm(state.astype(bf16), m[:W].astype(bf16)) + m[W:].astype(f32)


def kernel(
    tok_ref, kw_ref, q_ref, v_ref, g_ref, w0_ref, rate_ref,
    gt_ref, gkw_ref, gq_ref, gv_ref,
    tokcol, tok_t, ef_send, ef_recv, tot_send, tot_recv, nodes, state, x_send, wl,
    kf, invf, kbs, tks, tvs, ttks, ttzs, ubs, raw_all, part, zrecv,
    tok_ss, tok_rs, ef_ss, ef_rs, tot_ss, tot_rs, x_ss, wl_rs, ag_ss, ag_rs, z_ss, z_rs,
):
    me = lax.axis_index("seq")
    zme = lax.axis_index("head")
    y = me // ROW
    p = me % ROW
    x = p // NC
    core = p % NC
    row0 = y * ROW
    sib = me + 1 - 2 * core

    def seq_copy(src, dst, ss, rs, to):
        return pltpu.make_async_remote_copy(
            src_ref=src, dst_ref=dst, send_sem=ss, recv_sem=rs,
            device_id={"seq": to}, device_id_type=MESH,
        )

    def head_copy(src, dst, ss, rs, to):
        return pltpu.make_async_remote_copy(
            src_ref=src, dst_ref=dst, send_sem=ss, recv_sem=rs,
            device_id={"head": to}, device_id_type=MESH,
        )

    barrier = pltpu.get_barrier_semaphore()

    def greet_seq(off, c):
        pl.semaphore_signal(
            barrier, inc=1, device_id={"seq": (me + off) % NS}, device_id_type=MESH
        )
        return c

    def greet_head(off, c):
        pl.semaphore_signal(
            barrier, inc=1, device_id={"head": (zme + off) % NZ}, device_id_type=MESH
        )
        return c

    lax.fori_loop(1, NS, greet_seq, 0)
    lax.fori_loop(1, NZ, greet_head, 0)
    pl.semaphore_wait(barrier, NS - 1 + NZ - 1)

    def tok_copy(off):
        to = (me + off) % NS
        cols = pl.ds(pl.multiple_of(to * W, W), W)
        return seq_copy(tok_ref.at[:, cols], tokcol.at[me], tok_ss.at[off], tok_rs.at[off], to)

    def tok_start(off, c):
        tok_copy(off).start()
        return c

    lax.fori_loop(1, NS, tok_start, 0)

    kraw = mm(tok_ref[...], kw_ref[...])
    rates = [rate_base * rate_ref[h] for h in range(NH)]
    for h in range(NH):
        hs = slice(h * W, h * W + W)
        k, inv, kb, tk, tv, ttk, ttz, e0, f0, e1, f1 = local_maps(
            kraw[:, hs], v_ref[:, hs], q_ref[:, hs], g_ref[:, hs], rates[h]
        )
        kf[h] = k
        invf[h] = jnp.broadcast_to(inv, (W, W))
        kbs[h] = kb
        tks[h] = tk
        tvs[h] = tv
        ttks[h] = ttk
        ttzs[h] = ttz
        ef_send[0, h, :W] = e0
        ef_send[0, h, W:] = f0
        ef_send[1, h, :W] = e1
        ef_send[1, h, W:] = f1
        for role in range(2):
            slot = p if role == 0 else ROW - 1 - p
            here = NC * h + role

            @pl.when(p != here)
            def _():
                seq_copy(
                    ef_send.at[role, h], ef_recv.at[slot], ef_ss.at[role, h],
                    ef_rs.at[slot], row0 + here,
                ).start()

            @pl.when(p == here)
            def _():
                ef_recv[slot] = ef_send[role, h]

    own_slot = jnp.where(core == 0, p, ROW - 1 - p)
    for slot in range(ROW):
        frm = jnp.where(core == 0, slot, ROW - 1 - slot)

        @pl.when(slot != own_slot)
        def _():
            seq_copy(
                ef_send.at[0, 0], ef_recv.at[slot], ef_ss.at[0, 0], ef_rs.at[slot], row0 + frm
            ).wait_recv()

    for i in range(4):
        nodes[i] = join(ef_recv[2 * i], ef_recv[2 * i + 1])
    for i in range(2):
        nodes[4 + i] = join(nodes[2 * i], nodes[2 * i + 1])
    tot_send[...] = join(nodes[4], nodes[5]).astype(bf16)

    pos = jnp.where(core == 0, y, NY - 1 - y)
    for to_pos in range(1, NY):
        to_y = jnp.where(core == 0, to_pos, NY - 1 - to_pos)

        @pl.when(to_pos > pos)
        def _():
            seq_copy(
                tot_send, tot_recv.at[pos], tot_ss.at[to_pos], tot_rs.at[pos], to_y * ROW + p
            ).start()

    cols = pl.ds(pl.multiple_of(me * W, W), W)
    tokcol[me] = tok_ref[:, cols]

    def tok_wait(off, c):
        frm = (me + NS - off) % NS
        seq_copy(
            tokcol.at[frm], tokcol.at[frm], tok_ss.at[off], tok_rs.at[off], frm
        ).wait_recv()
        return c

    lax.fori_loop(1, NS, tok_wait, 0)

    def turn(s, c):
        tok_t[:, pl.ds(pl.multiple_of(s * W, W), W)] = tokcol[s].T
        return c

    lax.fori_loop(0, NS, turn, 0)

    state[...] = jnp.where(core == 0, w0_ref[x].T, 0.0)
    for j in range(NY - 1):
        frm_y = jnp.where(core == 0, j, NY - 1 - j)

        @pl.when(j < pos)
        def _():
            seq_copy(
                tot_send, tot_recv.at[j], tot_ss.at[0], tot_rs.at[j], frm_y * ROW + p
            ).wait_recv()
            state[...] = apply(state[...], tot_recv[j])

    xs = [None] * ROW
    xs[0] = state[...]
    xs[4] = apply(xs[0], nodes[4])
    xs[2] = apply(xs[0], nodes[0])
    xs[6] = apply(xs[4], nodes[2])
    for i in (0, 2, 4, 6):
        xs[i + 1] = apply(xs[i], ef_recv[i])
    for slot in range(ROW):
        x_send[slot] = xs[slot].astype(bf16)
        to = jnp.where(core == 0, slot, ROW - 1 - slot)

        @pl.when(to != p)
        def _():
            seq_copy(
                x_send.at[slot], wl.at[x, core], x_ss.at[slot], wl_rs.at[x, core], row0 + to
            ).start()

        @pl.when(to == p)
        def _():
            wl[x, core] = x_send[slot]

    def shard(yy, xx, cc):
        return (yy * NX + xx) * NC + cc

    def peer(axis, i):
        if axis == 0:
            return shard(y, (x + i) % NX, core)
        return shard((y + i) % NY, x, core)

    def ag_copy(half, s, sem, to):
        return seq_copy(
            raw_all.at[half, s], raw_all.at[half, s], ag_ss.at[half, sem], ag_rs.at[half, s], to
        )

    for half in range(2):
        for h in (2 * half, 2 * half + 1):
            hs = slice(h * W, h * W + W)
            for role in range(2):
                @pl.when(p != NC * h + role)
                def _():
                    seq_copy(
                        x_send.at[0], wl.at[h, role], x_ss.at[0], wl_rs.at[h, role],
                        row0 + NC * h + role,
                    ).wait_recv()

            bi, bj = batch_of()
            r = rates[h]
            w, l = wl[h, 0], wl[h, 1]
            q, g, kb = q_ref[:, hs], g_ref[:, hs], kbs[h]
            ub = (nt(tks[h], w) - tvs[h]).astype(bf16)
            yy = nt(ttks[h], l) + ttzs[h]
            yb = yy.astype(bf16)
            gv_ref[:, hs] = (r * yy).astype(bf16)
            ubs[h] = ub
            pm = jnp.where(bi <= bj, nt(ub, g), 0.0).astype(bf16)
            sm = (
                jnp.where(bi < bj, nt(ub, yb), 0.0) + jnp.where(bi > bj, nt(yb, ub), 0.0)
            ).astype(bf16)
            ka = -r * (mm(ub, l) + mm(yb, w) + mm(pm, q) - r * mm(sm, kb))
            k = kf[h]
            along = jnp.sum(k * ka, axis=1, keepdims=True)
            raw_all[half, me, :, (h % 2) * W:(h % 2) * W + W] = (
                (ka - k * along) * invf[h]
            ).astype(bf16)
        for i in range(1, 4):
            ag_copy(half, me, i, peer(half, i)).start()
        ag_copy(half, me, 16, sib).start()

    raw = jnp.concatenate([raw_all[0, me], raw_all[1, me]], axis=1)

    def z_copy(off):
        return head_copy(part.at[off], zrecv.at[off], z_ss.at[off], z_rs.at[off], (zme + off) % NZ)

    for off in (4, 3, 5, 2, 6, 1, 7, 0):
        to = (zme + off) % NZ
        rows = pl.ds(pl.multiple_of(to * NH * W, NH * W), NH * W)
        part[off] = nt(raw, kw_ref[rows, :]).astype(bf16)
        if off:
            z_copy(off).start()

    for half in range(2):
        for j in range(4):
            s = me if j == 0 else peer(half, j)
            if j:
                ag_copy(half, s, 0, sib).wait_recv()
                ag_copy(half, s, 16 + j, sib).start()
            for i in range(1, 4):
                ag_copy(half, s, 3 + 3 * j + i, peer(1 - half, i)).start()

    for h in range(NH):
        hs = slice(h * W, h * W + W)
        bi, bj = batch_of()
        g = g_ref[:, hs]
        low = jnp.where(bi >= bj, nt(g, ubs[h]), 0.0).astype(bf16)
        gq_ref[:, hs] = (mm(g, wl[h, 0]) - rates[h] * mm(low, kbs[h])).astype(bf16)

    for half in range(2):
        for j in range(4):
            for i in range(1, 4):
                if half == 0:
                    s = shard((y + i) % NY, (x + j) % NX, core)
                else:
                    s = shard((y + j) % NY, (x + i) % NX, core)
                ag_copy(half, s, 0, sib).wait_recv()
                ag_copy(half, s, 16 + 4 * i + j, sib).start()

    acc = part[0].astype(f32)
    for off in (1, 7, 2, 6, 3, 5, 4):
        z_copy(off).wait_recv()
        acc = acc + zrecv[off].astype(f32)
    gt_ref[...] = acc.astype(bf16)

    for half in range(2):
        def sib_wait(i, c, half=half):
            ag_copy(half, NC * i + 1 - core, 0, sib).wait_recv()
            return c

        lax.fori_loop(0, NS // NC, sib_wait, 0)
        gkw_ref[:, 2 * W * half:2 * W * (half + 1)] = mm(
            tok_t[...], raw_all[half].reshape(NS * W, 2 * W)
        )

    def tok_sent(off, c):
        tok_copy(off).wait_send()
        return c

    lax.fori_loop(1, NS, tok_sent, 0)
    for h in range(NH):
        for role in range(2):
            @pl.when(p != NC * h + role)
            def _():
                seq_copy(
                    ef_send.at[role, h], ef_recv.at[0], ef_ss.at[role, h], ef_rs.at[0], sib
                ).wait_send()
    for to_pos in range(1, NY):
        @pl.when(to_pos > pos)
        def _():
            seq_copy(tot_send, tot_recv.at[0], tot_ss.at[to_pos], tot_rs.at[0], sib).wait_send()
    for slot in range(ROW):
        @pl.when(slot != own_slot)
        def _():
            seq_copy(
                x_send.at[slot], wl.at[0, 0], x_ss.at[slot], wl_rs.at[0, 0], sib
            ).wait_send()
    for half in range(2):
        def ag_sent(i, c, half=half):
            ag_copy(half, me, i, sib).wait_send()
            return c

        lax.fori_loop(1, 32, ag_sent, 0)
    for off in range(1, NZ):
        z_copy(off).wait_send()


def per_device(tokens, key_weight, queries, values, grad_out, inner_start, head_rate):
    vmem = pl.BlockSpec(memory_space=pltpu.VMEM)
    smem = pl.BlockSpec(memory_space=pltpu.SMEM)
    cols = NH * W
    sem = pltpu.SemaphoreType.DMA
    return pl.pallas_call(
        kernel,
        out_shape=(
            jax.ShapeDtypeStruct((W, cols), bf16),
            jax.ShapeDtypeStruct((W, cols), f32),
            jax.ShapeDtypeStruct((W, cols), bf16),
            jax.ShapeDtypeStruct((W, cols), bf16),
        ),
        in_specs=[vmem] * 6 + [smem],
        out_specs=(vmem,) * 4,
        scratch_shapes=[
            pltpu.VMEM((NS, W, W), bf16),
            pltpu.VMEM((W, NS * W), bf16),
            pltpu.VMEM((2, NH, 2 * W, W), bf16),
            pltpu.VMEM((ROW, 2 * W, W), bf16),
            pltpu.VMEM((2 * W, W), bf16),
            pltpu.VMEM((NY, 2 * W, W), bf16),
            pltpu.VMEM((6, 2 * W, W), f32),
            pltpu.VMEM((W, W), f32),
            pltpu.VMEM((ROW, W, W), bf16),
            pltpu.VMEM((NH, 2, W, W), bf16),
            pltpu.VMEM((NH, W, W), f32),
            pltpu.VMEM((NH, W, W), f32),
            pltpu.VMEM((NH, W, W), bf16),
            pltpu.VMEM((NH, W, W), bf16),
            pltpu.VMEM((NH, W, W), f32),
            pltpu.VMEM((NH, W, W), bf16),
            pltpu.VMEM((NH, W, W), f32),
            pltpu.VMEM((NH, W, W), bf16),
            pltpu.VMEM((2, NS, W, 2 * W), bf16),
            pltpu.VMEM((NZ, W, cols), bf16),
            pltpu.VMEM((NZ, W, cols), bf16),
            sem((NS,)), sem((NS,)),
            sem((2, NH)), sem((ROW,)),
            sem((NY,)), sem((NY,)),
            sem((ROW,)), sem((NH, 2)),
            sem((2, NS)), sem((2, NS)),
            sem((NZ,)), sem((NZ,)),
        ],
        compiler_params=pltpu.CompilerParams(
            collective_id=0, has_side_effects=True, vmem_limit_bytes=48 * 1024 * 1024
        ),
        name="layer",
    )(tokens, key_weight, queries, values, grad_out, inner_start, head_rate)


def solution(mesh):
    placed = (
        P("seq", None),
        P(None, "head"),
        P("seq", "head"),
        P("seq", "head"),
        P("seq", "head"),
        P("head", None, None),
        P("head"),
    )
    return jax.shard_map(
        per_device,
        mesh=mesh,
        in_specs=placed,
        out_specs=(P("seq", "head"),) * 4,
        check_vma=False,
    )
```

time: 839 us -> 82.4 us (0.10)
  waiting for transfers between devices: 404 us -> 0 us
  starting transfers between devices: 232 us -> 0 us
  matrix products: 155 us -> 0 us
  Pallas kernels: 0 us -> 73.2 us
  between operations: 14.4 us -> 0.66 us
  local copies, waits for them, and re-layouts: 17.9 us -> 8.2 us
    ppermute x62 -> x0, waiting for transfers between devices: 263 us -> none  [from_behind(): return lax.ppermute(block, axis, route)]
    ppermute x62 -> x0, starting transfers between devices: 232 us -> none  [from_behind(): return lax.ppermute(block, axis, route)]
    dot_general x171 -> x0, matrix products: 155 us -> none  [the longest x40 45.9 us: outer(): return jnp.einsum('bhi,bhj->hij', keys_b, other, precision=best)]
    unnamed x3 -> x0, waiting for transfers between devices: 105 us -> none
    pallas_call x0 -> x1, Pallas kernels: none -> 73.2 us  [per_device(): pl.pallas_call(kernel, out_shape=(jax.ShapeDtypeStruct((W, cols), bf16),...]
    reduce_scatter x1 -> x0, waiting for transfers between devices: 36.2 us -> none  [per_device(): lax.psum_scatter(partial_sum.astype(jnp.bfloat16), 'head', scatter_dimens...]
  transfers between devices with their start and end apart: 64 -> 0, of which waited for: 64 -> 0; matrix products, arithmetic and copies ran while one was open for 1% -> 0% of each run, Pallas kernels for 0% -> 0%
where the time goes in v1:
time: 82.4 us; the launch traced here: 82.1 us
  Pallas kernels  73.2 us (89%)
  local copies, waits for them, and re-layouts  8.2 us (10%)
    pallas_call x1, Pallas kernels, per_device(): pl.pallas_call(kernel, out_shape=(jax.ShapeDtypeStruct((W, cols), bf16),...  73.2 us
    unnamed x16, local copies, waits for them, and re-layouts  8.2 us

profile of v1, /device:TPU:1, one launch (start us, length us, event | category | flops | bytes accessed | tf_op | source)
XLA Modules:
  0.0 82.1 jit_solution(15377768052701460958)
XLA Ops:
  0.6 0.0 copy-start
  0.6 1.2 %copy-done = bf16[128,4096]{1,0:T(8,128)(2,1)S(1)} copy-done((bf16[128,4096]{1,0:T(8,128)(2,1)S(1)}, bf16[128,4096]{1,0:T(8,128)(2,1)}, u32[]{:S(2)}) %copy-start) | copy-done | bytes 1048600
  1.9 0.0 copy-start.1
  1.9 0.9 %copy-done.1 = f32[4,128,128]{2,1,0:T(8,128)S(1)} copy-done((f32[4,128,128]{2,1,0:T(8,128)S(1)}, f32[4,128,128]{2,1,0:T(8,128)}, u32[]{:S(2)}) %copy-start.1) | copy-done | bytes 262168
  2.8 0.0 copy-start.2
  2.8 0.9 %copy-done.2 = bf16[128,512]{1,0:T(8,128)(2,1)S(1)} copy-done((bf16[128,512]{1,0:T(8,128)(2,1)S(1)}, bf16[128,512]{1,0:T(8,128)(2,1)}, u32[]{:S(2)}) %copy-start.2) | copy-done | bytes 131096
  3.7 0.0 copy-start.3
  3.7 0.9 %copy-done.3 = bf16[128,512]{1,0:T(8,128)(2,1)S(1)} copy-done((bf16[128,512]{1,0:T(8,128)(2,1)S(1)}, bf16[128,512]{1,0:T(8,128)(2,1)}, u32[]{:S(2)}) %copy-start.3) | copy-done | bytes 131096
  4.6 0.0 copy-start.4
  4.6 0.9 %copy-done.4 = bf16[128,512]{1,0:T(8,128)(2,1)S(1)} copy-done((bf16[128,512]{1,0:T(8,128)(2,1)S(1)}, bf16[128,512]{1,0:T(8,128)(2,1)}, u32[]{:S(2)}) %copy-start.4) | copy-done | bytes 131096
  5.5 0.0 copy-start.5
  5.5 0.7 copy-done.5
  6.2 73.2 %layer.1 = (bf16[128,512]{1,0:T(8,128)(2,1)S(1)}, f32[128,512]{1,0:T(8,128)S(1)}, bf16[128,512]{1,0:T(8,128)(2,1)S(1)}, bf16[128,512]{1,0:T(8,128)(2,1)S(1)}) custom-call(bf16[128,4096]{1,0:T(8,128)(2,1)S(1)} %copy-done, bf16[4096,512]{1,0:T(8,128)(2,1)} %kw_ref.1, bf16[128,512]{1,0:T(8,128)(2,1)S(1)} %copy-done.2, bf16[128,512]{1,0:T(8,128)(2,1)S(1)} %copy-done.3, ...), custom_call_target="tpu_custom_call" | custom-call | tf_op jit(solution)/shard_map/layer/pallas_call | solution.py:380
  79.4 0.7 copy.15
  80.1 0.7 copy.16
  80.8 0.7 copy.17
  81.4 0.7 copy.18
Async XLA Ops:
  0.6 1.2 %copy-start = (bf16[128,4096]{1,0:T(8,128)(2,1)S(1)}, bf16[128,4096]{1,0:T(8,128)(2,1)}, u32[]{:S(2)}) copy-start(bf16[128,4096]{1,0:T(8,128)(2,1)} %tok_ref.1) | copy-start | bytes 3145732
  1.9 0.9 %copy-start.1 = (f32[4,128,128]{2,1,0:T(8,128)S(1)}, f32[4,128,128]{2,1,0:T(8,128)}, u32[]{:S(2)}) copy-start(f32[4,128,128]{2,1,0:T(8,128)} %w0_ref.1) | copy-start | bytes 786436
  2.8 0.9 %copy-start.2 = (bf16[128,512]{1,0:T(8,128)(2,1)S(1)}, bf16[128,512]{1,0:T(8,128)(2,1)}, u32[]{:S(2)}) copy-start(bf16[128,512]{1,0:T(8,128)(2,1)} %q_ref.1) | copy-start | bytes 393220
  3.7 0.9 %copy-start.3 = (bf16[128,512]{1,0:T(8,128)(2,1)S(1)}, bf16[128,512]{1,0:T(8,128)(2,1)}, u32[]{:S(2)}) copy-start(bf16[128,512]{1,0:T(8,128)(2,1)} %v_ref.1) | copy-start | bytes 393220
  4.6 0.9 %copy-start.4 = (bf16[128,512]{1,0:T(8,128)(2,1)S(1)}, bf16[128,512]{1,0:T(8,128)(2,1)}, u32[]{:S(2)}) copy-start(bf16[128,512]{1,0:T(8,128)(2,1)} %g_ref.1) | copy-start | bytes 393220
  5.5 0.7 copy-start.5

commit v2 on v1

v2 whole, which is shorter than its diff:
```python
import jax
import jax.numpy as jnp
from jax import lax
from jax.experimental import pallas as pl
from jax.experimental.pallas import tpu as pltpu
from jax.sharding import PartitionSpec as P

MESH = pl.DeviceIdType.MESH
bf16 = jnp.bfloat16
f32 = jnp.float32
rate_base = 0.1
norm_eps = 1e-06
W = 128
NH = 4
NX, NY, NC = 4, 4, 2
ROW = NX * NC
NS = ROW * NY
NZ = 8
TZ = W // NZ
KW_PARTS = 4


def mm(a, b):
    return lax.dot_general(a, b, (((1,), (0,)), ((), ())), preferred_element_type=f32)


def nt(a, b):
    return lax.dot_general(a, b, (((1,), (1,)), ((), ())), preferred_element_type=f32)


def tn(a, b):
    return lax.dot_general(a, b, (((0,), (0,)), ((), ())), preferred_element_type=f32)


def batch_of():
    rows = lax.broadcasted_iota(jnp.int32, (W, W), 0) >> 4
    cols = lax.broadcasted_iota(jnp.int32, (W, W), 1) >> 4
    return rows, cols


def local_maps(kraw, v, q, g, r):
    bi, bj = batch_of()
    inv = lax.rsqrt(jnp.sum(kraw * kraw, axis=1, keepdims=True) + norm_eps)
    k = kraw * inv
    kb = k.astype(bf16)
    m = r * nt(kb, kb)
    x1 = jnp.where(((bi >> 1) == (bj >> 1)) & (bi > bj), m, 0.0)
    x2 = jnp.where(((bi >> 2) == (bj >> 2)) & ((bi >> 1) > (bj >> 1)), m, 0.0)
    x3 = jnp.where((bi >> 2) > (bj >> 2), m, 0.0)
    rows = lax.broadcasted_iota(jnp.int32, (W, W), 0)
    cols = lax.broadcasted_iota(jnp.int32, (W, W), 1)
    t1 = jnp.where(rows == cols, 1.0, 0.0) - x1
    t1b = t1.astype(bf16)
    t2 = t1 - mm(mm(t1b, x2.astype(bf16)).astype(bf16), t1b)
    t2b = t2.astype(bf16)
    t3 = t2 - mm(mm(t2b, x3.astype(bf16)).astype(bf16), t2b)
    tb = t3.astype(bf16)
    tk = mm(tb, kb).astype(bf16)
    tv = mm(tb, v)
    z = mm(jnp.where(bi <= bj, nt(kb, q), 0.0).astype(bf16), g).astype(bf16)
    ttk = tn(tb, kb).astype(bf16)
    ttz = tn(tb, z)
    e0 = (-r * tn(tk, kb)).astype(bf16)
    f0 = (r * tn(tv.astype(bf16), kb)).astype(bf16)
    e1 = (-r * tn(kb, tk)).astype(bf16)
    f1 = (tn(g, q) - r * tn(ttz.astype(bf16), kb)).astype(bf16)
    return k, inv, kb, tk, tv, ttk, ttz, e0, f0, e1, f1


def join(a, b):
    return a.astype(f32) + b.astype(f32) + mm(a.astype(bf16), b[:W].astype(bf16))


def apply(state, m):
    return state + mm(state.astype(bf16), m[:W].astype(bf16)) + m[W:].astype(f32)


def kernel(
    tok_hbm, kw_hbm, q_hbm, v_hbm, g_hbm, w0_hbm, rate_ref,
    gt_ref, gkw_ref, gq_ref, gv_ref,
    tok_ref, kw_ref, q_ref, v_ref, g_ref, w0_ref,
    tokcol, tok_t, ef_send, ef_recv, tot_send, tot_recv, nodes, state, x_send, wl,
    kf, invf, kbs, tks, tvs, ttks, ttzs, ubs, raw_all, zs, zr,
    in_s, tok_ss, tok_rs, tz_ss, tz_rs, ef_ss, ef_rs, tot_ss, tot_rs, x_ss, x_rs,
    ag_ss, ag_rs, sib_rs, z_ss, z_rs,
):
    me = lax.axis_index("seq")
    zme = lax.axis_index("head")
    y = me // ROW
    p = me % ROW
    x = p // NC
    core = p % NC
    row0 = y * ROW
    sib = me + 1 - 2 * core

    def seq_copy(src, dst, ss, rs, to):
        return pltpu.make_async_remote_copy(
            src_ref=src, dst_ref=dst, send_sem=ss, recv_sem=rs,
            device_id={"seq": to}, device_id_type=MESH,
        )

    def head_copy(src, dst, ss, rs, to):
        return pltpu.make_async_remote_copy(
            src_ref=src, dst_ref=dst, send_sem=ss, recv_sem=rs,
            device_id={"head": to}, device_id_type=MESH,
        )

    deep = kw_ref.shape[0] // KW_PARTS
    loads = [pltpu.make_async_copy(tok_hbm, tok_ref, in_s.at[0])]
    for i in range(KW_PARTS):
        rows = pl.ds(i * deep, deep)
        loads.append(pltpu.make_async_copy(kw_hbm.at[rows], kw_ref.at[rows], in_s.at[1 + i]))
    for i, (src, dst) in enumerate(
        ((q_hbm, q_ref), (v_hbm, v_ref), (g_hbm, g_ref), (w0_hbm, w0_ref))
    ):
        loads.append(pltpu.make_async_copy(src, dst, in_s.at[1 + KW_PARTS + i]))
    for load in loads:
        load.start()

    barrier = pltpu.get_barrier_semaphore()

    def greet_seq(off, c):
        pl.semaphore_signal(
            barrier, inc=1, device_id={"seq": (me + off) % NS}, device_id_type=MESH
        )
        return c

    lax.fori_loop(1, NS, greet_seq, 0)
    up, down = (zme + 1) % NZ, (zme + NZ - 1) % NZ
    for to in (up, down):
        pl.semaphore_signal(barrier, inc=1, device_id={"head": to}, device_id_type=MESH)

    loads[0].wait()
    kraw = None
    for i in range(KW_PARTS):
        loads[1 + i].wait()
        rows = slice(i * deep, (i + 1) * deep)
        prod = mm(tok_ref[:, rows], kw_ref[rows, :])
        kraw = prod if kraw is None else kraw + prod
    for load in loads[1 + KW_PARTS:]:
        load.wait()
    rates = [rate_base * rate_ref[h] for h in range(NH)]
    for h in range(NH):
        hs = slice(h * W, h * W + W)
        k, inv, kb, tk, tv, ttk, ttz, e0, f0, e1, f1 = local_maps(
            kraw[:, hs], v_ref[:, hs], q_ref[:, hs], g_ref[:, hs], rates[h]
        )
        kf[h] = k
        invf[h] = jnp.broadcast_to(inv, (W, W))
        kbs[h] = kb
        tks[h] = tk
        tvs[h] = tv
        ttks[h] = ttk
        ttzs[h] = ttz
        ef_send[0, h, :W] = e0
        ef_send[0, h, W:] = f0
        ef_send[1, h, :W] = e1
        ef_send[1, h, W:] = f1
        if h == 0:
            pl.semaphore_wait(barrier, NS - 1 + 2)
        for role in range(2):
            slot = p if role == 0 else ROW - 1 - p
            here = NC * h + role

            @pl.when(p != here)
            def _():
                seq_copy(
                    ef_send.at[role, h], ef_recv.at[slot], ef_ss, ef_rs, row0 + here
                ).start()

            @pl.when(p == here)
            def _():
                ef_recv[slot] = ef_send[role, h]

    my_slot = (core * NY + y) * NX + x
    part_rows = pl.ds(pl.multiple_of(zme * TZ, TZ), TZ)

    def tok_start(off, c):
        to = (me + off) % NS
        cols = pl.ds(pl.multiple_of(to * W, W), W)
        seq_copy(
            tok_ref.at[part_rows, cols], tokcol.at[zme, my_slot], tok_ss, tok_rs, to
        ).start()
        return c

    lax.fori_loop(1, NS, tok_start, 0)
    tokcol[zme, my_slot] = tok_ref[part_rows, pl.ds(pl.multiple_of(me * W, W), W)]
    tok_all = tokcol.at[0, pl.ds(0, NS - 1)]
    tok_sum = seq_copy(tok_all, tok_all, tok_ss, tok_rs, sib)

    def tz(dist, way, wait=False):
        blk = (zme + NZ - way * dist) % NZ
        ref = tokcol.at[blk]
        if dist == 3:
            ref = tokcol.at[blk, pl.ds(0 if way == 1 else NS // 2, NS // 2)]
        sem = tz_rs.at[2 * dist + (way == 1)]
        return head_copy(ref, ref, tz_ss, sem, up if way == 1 else down)

    def tz_arrived(dist, way):
        blk = (zme + NZ - way * dist) % NZ
        ref = tokcol.at[blk]
        if dist == 4:
            ref = tokcol.at[blk, pl.ds(0 if way == 1 else NS // 2, NS // 2)]
        sem = tz_rs.at[2 * (dist - 1) + (way == 1)]
        head_copy(ref, ref, tz_ss, sem, up).wait_recv()

    own_slot = jnp.where(core == 0, p, ROW - 1 - p)
    some = ef_recv.at[pl.ds(0, ROW - 1)]
    ef_sum = seq_copy(some, some, ef_ss, ef_rs, sib)
    ef_sum.wait_recv()
    for i in range(4):
        nodes[i] = join(ef_recv[2 * i], ef_recv[2 * i + 1])
    for i in range(2):
        nodes[4 + i] = join(nodes[2 * i], nodes[2 * i + 1])
    tot_send[...] = join(nodes[4], nodes[5]).astype(bf16)

    pos = jnp.where(core == 0, y, NY - 1 - y)
    for to_pos in range(1, NY):
        to_y = jnp.where(core == 0, to_pos, NY - 1 - to_pos)

        @pl.when(to_pos > pos)
        def _():
            seq_copy(
                tot_send, tot_recv.at[pos], tot_ss.at[to_pos], tot_rs.at[pos], to_y * ROW + p
            ).start()

    tok_sum.wait_recv()
    tz(0, 1).start()
    tz(0, -1).start()

    state[...] = jnp.where(core == 0, w0_ref[x].T, 0.0)
    for j in range(NY - 1):
        frm_y = jnp.where(core == 0, j, NY - 1 - j)

        @pl.when(j < pos)
        def _():
            seq_copy(
                tot_send, tot_recv.at[j], tot_ss.at[0], tot_rs.at[j], frm_y * ROW + p
            ).wait_recv()
            state[...] = apply(state[...], tot_recv[j])

    xs = [None] * ROW
    xs[0] = state[...]
    xs[4] = apply(xs[0], nodes[4])
    xs[2] = apply(xs[0], nodes[0])
    xs[6] = apply(xs[4], nodes[2])
    for i in (0, 2, 4, 6):
        xs[i + 1] = apply(xs[i], ef_recv[i])
    for slot in range(ROW):
        x_send[slot] = xs[slot].astype(bf16)
        to = jnp.where(core == 0, slot, ROW - 1 - slot)

        @pl.when(to != p)
        def _():
            seq_copy(x_send.at[slot], wl.at[2 * x + core], x_ss, x_rs, row0 + to).start()

        @pl.when(to == p)
        def _():
            wl[2 * x + core] = x_send[slot]

    for way in (1, -1):
        tz_arrived(1, way)
        tz(1, way).start()
    some_x = wl.at[pl.ds(0, ROW - 1)]
    x_sum = seq_copy(some_x, some_x, x_ss, x_rs, sib)
    x_sum.wait_recv()

    mine = ((x, y), (y, x))

    def spot(half, da, db):
        a, b = mine[half]
        return core * 4 + (b + db) % 4, (a + da) % 4

    def device(half, da, db):
        a, b = mine[half]
        a, b = (a + da) % 4, (b + db) % 4
        xx, yy = (a, b) if half == 0 else (b, a)
        return (yy * NX + xx) * NC + core

    def shard(half, da, db, piece=None):
        g, a = spot(half, da, db)
        if piece is None:
            return raw_all.at[half, g, a]
        return raw_all.at[half, g, a, pl.ds(piece * (W // 2), W // 2)]

    def ag_sem(half, da, kind):
        return ag_rs.at[half, 4 * (da % 4) + kind]

    def ag_send(half, da, db, leg, way, piece=None):
        ref = shard(half, da, db, piece)
        to = device(half, way, 0) if leg == 0 else device(half, 0, way)
        kind = (0 if way == 1 else 1) if piece is None else 2 + piece
        sem = ag_rs.at[half, 16 + kind] if leg == 0 else ag_sem(half, da, kind)
        seq_copy(ref, ref, ag_ss.at[half], sem, to).start()

    def ag_wait(half, da, db, leg, kind):
        ref = shard(half, da, db, kind - 2 if kind >= 2 else None)
        sem = ag_rs.at[half, 16 + kind] if leg == 0 else ag_sem(half, da, kind)
        seq_copy(ref, ref, ag_ss.at[half], sem, sib).wait_recv()

    def first_leg_on(half):
        ag_wait(half, -1, 0, 0, 0)
        ag_send(half, -1, 0, 0, 1, 0)
        ag_wait(half, 1, 0, 0, 1)
        ag_send(half, 1, 0, 0, -1, 1)

    def second_leg(half, da):
        ag_send(half, da, 0, 1, 1)
        ag_send(half, da, 0, 1, -1)

    def second_leg_on(half, da):
        ag_wait(half, da, -1, 1, 0)
        ag_send(half, da, -1, 1, 1, 0)
        ag_wait(half, da, 1, 1, 1)
        ag_send(half, da, 1, 1, -1, 1)

    def sib_copy(half, db, cc):
        b = mine[half][1]
        ref = raw_all.at[half, cc * 4 + (b + db) % 4]
        return seq_copy(ref, ref, ag_ss.at[half], sib_rs.at[half, db % 4], sib)

    for half in range(2):
        raws = []
        for h in (2 * half, 2 * half + 1):
            hs = slice(h * W, h * W + W)
            bi, bj = batch_of()
            r = rates[h]
            w, l = wl[2 * h], wl[2 * h + 1]
            q, g, kb = q_ref[:, hs], g_ref[:, hs], kbs[h]
            ub = (nt(tks[h], w) - tvs[h]).astype(bf16)
            yy = nt(ttks[h], l) + ttzs[h]
            yb = yy.astype(bf16)
            gv_ref[:, hs] = (r * yy).astype(bf16)
            ubs[h] = ub
            pm = jnp.where(bi <= bj, nt(ub, g), 0.0).astype(bf16)
            sm = (
                jnp.where(bi < bj, nt(ub, yb), 0.0) + jnp.where(bi > bj, nt(yb, ub), 0.0)
            ).astype(bf16)
            ka = -r * (mm(ub, l) + mm(yb, w) + mm(pm, q) - r * mm(sm, kb))
            k = kf[h]
            along = jnp.sum(k * ka, axis=1, keepdims=True)
            raws.append(((ka - k * along) * invf[h]).astype(bf16))
        g, a = spot(half, 0, 0)
        raw_all[half, g, a] = jnp.concatenate(raws, axis=1)
        ag_send(half, 0, 0, 0, 1)
        ag_send(half, 0, 0, 0, -1)

    raw = jnp.concatenate(
        [raw_all[half, spot(half, 0, 0)[0], spot(half, 0, 0)[1]] for half in range(2)], axis=1
    )

    def part(off):
        to = (zme + off) % NZ
        rows = pl.ds(pl.multiple_of(to * NH * W, NH * W), NH * W)
        out = nt(raw, kw_ref[rows, :])
        zs[off, 0] = out[:, :2 * W].astype(bf16)
        zs[off, 1] = out[:, 2 * W:].astype(bf16)

    def z_copy(way, n, half):
        off = 4 - n if way == 0 else (4 + n) % NZ
        return head_copy(
            zs.at[off, half], zr.at[way, n, half], z_ss, z_rs.at[way, 2 * n + half],
            up if way == 0 else down,
        )

    def z_add(way, n, half):
        off = 4 - n if way == 0 else (4 + n) % NZ
        z_copy(way, n - 1, half).wait_recv()
        zs[off, half] = (
            zs[off, half].astype(f32) + zr[way, n - 1, half].astype(f32)
        ).astype(bf16)
        z_copy(way, n, half).start()

    part(4)
    z_copy(0, 0, 0).start()
    z_copy(1, 0, 1).start()
    part(3)
    z_copy(0, 1, 1).start()
    part(5)
    z_copy(1, 1, 0).start()

    for half in range(2):
        second_leg(half, 0)
        first_leg_on(half)
        second_leg(half, -1)
        second_leg(half, 1)

    part(2)
    part(6)
    z_add(0, 1, 0)
    z_add(1, 1, 1)
    z_add(0, 2, 1)
    z_add(1, 2, 0)
    for half in range(2):
        ag_wait(half, 2, 0, 0, 2)
        ag_wait(half, 2, 0, 0, 3)
        second_leg(half, 2)
        sib_copy(half, 0, core).start()
    part(1)
    part(7)
    z_add(0, 2, 0)
    z_add(1, 2, 1)
    for half in range(2):
        second_leg_on(half, 0)
    z_add(0, 3, 1)
    z_add(1, 3, 0)
    part(0)
    for half in range(2):
        second_leg_on(half, -1)
    z_add(0, 3, 0)
    z_add(1, 3, 1)
    for half in range(2):
        second_leg_on(half, 1)
    for half in range(2):
        second_leg_on(half, 2)
        sib_copy(half, -1, core).start()
        sib_copy(half, 1, core).start()

    for dist in (2, 3):
        for way in (1, -1):
            tz_arrived(dist, way)
            tz(dist, way).start()
    for way in (1, -1):
        tz_arrived(4, way)

    def turn(b, c):
        for cc in range(NC):
            for a in range(4):
                t = tokcol[:, (cc * NY + b) * NX + a].reshape(W, W).T
                tok_t[0, cc, b, :, a * W:a * W + W] = t
                tok_t[1, cc, a, :, pl.ds(pl.multiple_of(b * W, W), W)] = t
        return c

    lax.fori_loop(0, 4, turn, 0)

    for h in range(NH):
        hs = slice(h * W, h * W + W)
        bi, bj = batch_of()
        g = g_ref[:, hs]
        low = jnp.where(bi >= bj, nt(g, ubs[h]), 0.0).astype(bf16)
        gq_ref[:, hs] = (mm(g, wl[2 * h]) - rates[h] * mm(low, kbs[h])).astype(bf16)

    for half in range(2):
        z_copy(0, 3, half).wait_recv()
        z_copy(1, 3, half).wait_recv()
        gt_ref[:, 2 * W * half:2 * W * (half + 1)] = (
            zs[0, half].astype(f32) + zr[0, 3, half].astype(f32) + zr[1, 3, half].astype(f32)
        ).astype(bf16)

    def product(half, db, cc):
        b = (mine[half][1] + db) % 4
        return mm(tok_t[half, cc, b], raw_all[half, cc * 4 + b].reshape(4 * W, 2 * W))

    accs = [
        product(half, 0, core) + product(half, -1, core) + product(half, 1, core)
        for half in range(2)
    ]
    for half in range(2):
        for da in (0, -1, 1, 2):
            ag_wait(half, da, 2, 1, 2)
            ag_wait(half, da, 2, 1, 3)
        sib_copy(half, 2, core).start()
        accs[half] = accs[half] + product(half, 2, core)
    for half in range(2):
        for db in (0, -1, 1, 2):
            sib_copy(half, db, 1 - core).wait_recv()
            accs[half] = accs[half] + product(half, db, 1 - core)
        gkw_ref[:, 2 * W * half:2 * W * (half + 1)] = accs[half]

    tok_sum.wait_send()
    head_copy(tokcol.at[pl.ds(0, 7)], tokcol.at[pl.ds(0, 7)], tz_ss, tz_rs.at[0], up).wait_send()
    ef_sum.wait_send()
    for to_pos in range(1, NY):
        @pl.when(to_pos > pos)
        def _():
            seq_copy(tot_send, tot_recv.at[0], tot_ss.at[to_pos], tot_rs.at[0], sib).wait_send()
    x_sum.wait_send()
    for half in range(2):
        ref = kw_ref.at[pl.ds(0, 31 * W // 2)]
        seq_copy(ref, ref, ag_ss.at[half], sib_rs.at[half, 0], sib).wait_send()
    some_z = zs.at[pl.ds(0, 7)]
    head_copy(some_z, some_z, z_ss, z_rs.at[0, 0], up).wait_send()


def hand_over(a0, a1, a2, a3, b0, b1, b2, b3):
    for a, b in ((a0, b0), (a1, b1), (a2, b2), (a3, b3)):
        b[...] = a[...]


def per_device(tokens, key_weight, queries, values, grad_out, inner_start, head_rate):
    vmem = pl.BlockSpec(memory_space=pltpu.VMEM)
    smem = pl.BlockSpec(memory_space=pltpu.SMEM)
    anywhere = pl.BlockSpec(memory_space=pl.ANY)
    cols = NH * W
    sem = pltpu.SemaphoreType.DMA
    shapes = (
        jax.ShapeDtypeStruct((W, cols), bf16),
        jax.ShapeDtypeStruct((W, cols), f32),
        jax.ShapeDtypeStruct((W, cols), bf16),
        jax.ShapeDtypeStruct((W, cols), bf16),
    )
    outs = pl.pallas_call(
        kernel,
        out_shape=shapes,
        in_specs=[anywhere] * 6 + [smem],
        out_specs=(vmem,) * 4,
        scratch_shapes=[
            pltpu.VMEM(tokens.shape, bf16),
            pltpu.VMEM(key_weight.shape, bf16),
            pltpu.VMEM((W, cols), bf16),
            pltpu.VMEM((W, cols), bf16),
            pltpu.VMEM((W, cols), bf16),
            pltpu.VMEM((NH, W, W), f32),
            pltpu.VMEM((NZ, NS, TZ, W), bf16),
            pltpu.VMEM((2, NC, 4, W, 4 * W), bf16),
            pltpu.VMEM((2, NH, 2 * W, W), bf16),
            pltpu.VMEM((ROW, 2 * W, W), bf16),
            pltpu.VMEM((2 * W, W), bf16),
            pltpu.VMEM((NY, 2 * W, W), bf16),
            pltpu.VMEM((6, 2 * W, W), f32),
            pltpu.VMEM((W, W), f32),
            pltpu.VMEM((ROW, W, W), bf16),
            pltpu.VMEM((2 * NH, W, W), bf16),
            pltpu.VMEM((NH, W, W), f32),
            pltpu.VMEM((NH, W, W), f32),
            pltpu.VMEM((NH, W, W), bf16),
            pltpu.VMEM((NH, W, W), bf16),
            pltpu.VMEM((NH, W, W), f32),
            pltpu.VMEM((NH, W, W), bf16),
            pltpu.VMEM((NH, W, W), f32),
            pltpu.VMEM((NH, W, W), bf16),
            pltpu.VMEM((2, NC * 4, 4, W, 2 * W), bf16),
            pltpu.VMEM((NZ, 2, W, 2 * W), bf16),
            pltpu.VMEM((2, 4, 2, W, 2 * W), bf16),
            sem((5 + KW_PARTS,)),
            sem, sem,
            sem, sem((NZ,)),
            sem, sem,
            sem((NY,)), sem((NY,)),
            sem, sem,
            sem((2,)), sem((2, 20)), sem((2, 4)),
            sem, sem((2, 8)),
        ],
        compiler_params=pltpu.CompilerParams(
            collective_id=0, has_side_effects=True, vmem_limit_bytes=56 * 1024 * 1024
        ),
        name="layer",
    )(tokens, key_weight, queries, values, grad_out, inner_start, head_rate)
    return pl.pallas_call(
        hand_over,
        out_shape=shapes,
        in_specs=[vmem] * 4,
        out_specs=(vmem,) * 4,
        name="hand_over",
    )(*outs)


def solution(mesh):
    placed = (
        P("seq", None),
        P(None, "head"),
        P("seq", "head"),
        P("seq", "head"),
        P("seq", "head"),
        P("head", None, None),
        P("head"),
    )
    return jax.shard_map(
        per_device,
        mesh=mesh,
        in_specs=placed,
        out_specs=(P("seq", "head"),) * 4,
        check_vma=False,
    )
```

time: 82.4 us -> 64.7 us (0.79)
  Pallas kernels: 73.2 us -> 63.9 us
  local copies, waits for them, and re-layouts: 8.2 us -> 0 us
    pallas_call x1 -> x2, Pallas kernels: 73.2 us -> 63.9 us  [the longest x1 62 us: per_device(): pl.pallas_call(kernel, out_shape=shapes, in_specs=[anywhere] * 6 + [smem]...]
    unnamed x16 -> x0, local copies, waits for them, and re-layouts: 8.2 us -> none
where the time goes in v2:
time: 64.7 us; the launch traced here: 64.6 us
  Pallas kernels  63.9 us (99%)
    pallas_call x1, Pallas kernels, per_device(): pl.pallas_call(kernel, out_shape=shapes, in_specs=[anywhere] * 6 + [smem]...  62 us
    pallas_call x1, Pallas kernels, per_device(): pl.pallas_call(hand_over, out_shape=shapes, in_specs=[vmem] * 4, out_spec...  1.96 us

profile of v2, /device:TPU:1, one launch (start us, length us, event | category | flops | bytes accessed | tf_op | source)
XLA Modules:
  0.0 64.6 jit_solution(14557836129404751510)
XLA Ops:
  0.6 62.0 %layer.1 = (bf16[128,512]{1,0:T(8,128)(2,1)}, f32[128,512]{1,0:T(8,128)}, bf16[128,512]{1,0:T(8,128)(2,1)}, bf16[128,512]{1,0:T(8,128)(2,1)}) custom-call(bf16[128,4096]{1,0:T(8,128)(2,1)} %tok_hbm.1, bf16[4096,512]{1,0:T(8,128)(2,1)} %kw_hbm.1, bf16[128,512]{1,0:T(8,128)(2,1)} %q_hbm.1, bf16[128,512]{1,0:T(8,128)(2,1)} %v_hbm.1, bf16[128,512]{1,0:T(8,128)(2,1)} %g_hbm.1, ...), custom_call_target="tpu_custom_call" | custom-call | tf_op jit(solution)/shard_map/layer/pallas_call | solution.py:502
  62.6 2.0 %hand_over.1 = (bf16[128,512]{1,0:T(8,128)(2,1)}, f32[128,512]{1,0:T(8,128)}, bf16[128,512]{1,0:T(8,128)(2,1)}, bf16[128,512]{1,0:T(8,128)(2,1)}) custom-call(bf16[128,512]{1,0:T(8,128)(2,1)} %get-tuple-element.8.a0, f32[128,512]{1,0:T(8,128)} %get-tuple-element.9.a1, bf16[128,512]{1,0:T(8,128)(2,1)} %get-tuple-element.10.a2, ...), custom_call_target="tpu_custom_call" | custom-call | tf_op jit(solution)/shard_map/hand_over/pallas_call | solution.py:549

commit v3 on v2

v3 whole, which is shorter than its diff:
```python
import jax
import jax.numpy as jnp
from jax import lax
from jax.experimental import pallas as pl
from jax.experimental.pallas import tpu as pltpu
from jax.sharding import PartitionSpec as P

MESH = pl.DeviceIdType.MESH
bf16 = jnp.bfloat16
f32 = jnp.float32
rate_base = 0.1
norm_eps = 1e-06
W = 128
NH = 4
NX, NY, NC = 4, 4, 2
ROW = NX * NC
NZ = 8
KW_PARTS = 4


def mm(a, b):
    return lax.dot_general(a, b, (((1,), (0,)), ((), ())), preferred_element_type=f32)


def nt(a, b):
    return lax.dot_general(a, b, (((1,), (1,)), ((), ())), preferred_element_type=f32)


def tn(a, b):
    return lax.dot_general(a, b, (((0,), (0,)), ((), ())), preferred_element_type=f32)


def batch_of():
    rows = lax.broadcasted_iota(jnp.int32, (W, W), 0) >> 4
    cols = lax.broadcasted_iota(jnp.int32, (W, W), 1) >> 4
    return rows, cols


def local_maps(kraw, v, q, g, r):
    bi, bj = batch_of()
    inv = lax.rsqrt(jnp.sum(kraw * kraw, axis=1, keepdims=True) + norm_eps)
    k = kraw * inv
    kb = k.astype(bf16)
    m = r * nt(kb, kb)
    x1 = jnp.where(((bi >> 1) == (bj >> 1)) & (bi > bj), m, 0.0)
    x2 = jnp.where(((bi >> 2) == (bj >> 2)) & ((bi >> 1) > (bj >> 1)), m, 0.0)
    x3 = jnp.where((bi >> 2) > (bj >> 2), m, 0.0)
    rows = lax.broadcasted_iota(jnp.int32, (W, W), 0)
    cols = lax.broadcasted_iota(jnp.int32, (W, W), 1)
    t1 = jnp.where(rows == cols, 1.0, 0.0) - x1
    t1b = t1.astype(bf16)
    t2 = t1 - mm(mm(t1b, x2.astype(bf16)).astype(bf16), t1b)
    t2b = t2.astype(bf16)
    t3 = t2 - mm(mm(t2b, x3.astype(bf16)).astype(bf16), t2b)
    tb = t3.astype(bf16)
    tk = mm(tb, kb).astype(bf16)
    tv = mm(tb, v)
    z = mm(jnp.where(bi <= bj, nt(kb, q), 0.0).astype(bf16), g).astype(bf16)
    ttk = tn(tb, kb).astype(bf16)
    ttz = tn(tb, z)
    e0 = (-r * tn(tk, kb)).astype(bf16)
    f0 = (r * tn(tv.astype(bf16), kb)).astype(bf16)
    e1 = (-r * tn(kb, tk)).astype(bf16)
    f1 = (tn(g, q) - r * tn(ttz.astype(bf16), kb)).astype(bf16)
    return k, inv, kb, tk, tv, ttk, ttz, e0, f0, e1, f1


def join(a, b):
    return a.astype(f32) + b.astype(f32) + mm(a.astype(bf16), b[:W].astype(bf16))


def apply(state, m):
    return state + mm(state.astype(bf16), m[:W].astype(bf16)) + m[W:].astype(f32)


def kernel(
    tok_hbm, kw_hbm, q_hbm, v_hbm, g_hbm, w0_hbm, rate_ref,
    gt_ref, gkw_ref, gq_ref, gv_ref,
    tok_ref, kw_ref, q_ref, v_ref, g_ref, w0_ref, kraw_ref,
    tokcol, tok_t, maps, sib_maps, first, chip_maps, ef_recv, tot_send, tot_recv, nodes,
    state, x_send, x_in, x_sib, wl,
    kf, invf, kbs, tks, tvs, ttks, ttzs, ubs, raw_all, psum, rs_s, rs_r, zs, zr,
    in_s, tok_ss, tok_rs, tz_ss, tz_rs, sm_ss, sm_rs, ef_ss, ef_rs, tot_ss, tot_rs,
    x_ss, x_rs, xs_ss, xs_rs, ag_ss, ag_rs, sib_rs, rs_ss, rs_rs, z_ss, z_rs,
):
    me = lax.axis_index("seq")
    zme = lax.axis_index("head")
    y = me // ROW
    p = me % ROW
    x = p // NC
    core = p % NC
    sib = me + 1 - 2 * core
    hands = x // 2 == core

    def dev(yy, xx, cc):
        return (yy * NX + xx) * NC + cc

    def seq_copy(src, dst, ss, rs, to):
        return pltpu.make_async_remote_copy(
            src_ref=src, dst_ref=dst, send_sem=ss, recv_sem=rs,
            device_id={"seq": to}, device_id_type=MESH,
        )

    def head_copy(src, dst, ss, rs, to):
        return pltpu.make_async_remote_copy(
            src_ref=src, dst_ref=dst, send_sem=ss, recv_sem=rs,
            device_id={"head": to}, device_id_type=MESH,
        )

    deep = kw_ref.shape[0] // KW_PARTS
    loads = [pltpu.make_async_copy(tok_hbm, tok_ref, in_s.at[0])]
    for i in range(KW_PARTS):
        rows = pl.ds(i * deep, deep)
        loads.append(pltpu.make_async_copy(kw_hbm.at[rows], kw_ref.at[rows], in_s.at[1 + i]))
    for i, (src, dst) in enumerate(
        ((q_hbm, q_ref), (v_hbm, v_ref), (g_hbm, g_ref), (w0_hbm, w0_ref))
    ):
        loads.append(pltpu.make_async_copy(src, dst, in_s.at[1 + KW_PARTS + i]))
    for load in loads:
        load.start()

    barrier = pltpu.get_barrier_semaphore()

    def greet_seq(to):
        pl.semaphore_signal(barrier, inc=1, device_id={"seq": to}, device_id_type=MESH)

    for i in range(1, ROW):
        greet_seq(y * ROW + (p + i) % ROW)
    for i in range(1, NY):
        for cc in range(NC):
            greet_seq(dev((y + i) % NY, x, cc))
    z_at = [(zme + i) % NZ for i in range(NZ)]
    for i in (1, 2, 6, 7):
        pl.semaphore_signal(
            barrier, inc=1, device_id={"head": z_at[i]}, device_id_type=MESH
        )
    partners = ROW - 1 + NC * (NY - 1) + 4

    loads[0].wait()
    kraw = None
    for i in range(KW_PARTS):
        loads[1 + i].wait()
        rows = slice(i * deep, (i + 1) * deep)
        prod = mm(tok_ref[:, rows], kw_ref[rows, :])
        kraw = prod if kraw is None else kraw + prod
    kraw_ref[...] = kraw
    for load in loads[1 + KW_PARTS:]:
        load.wait()
    for i in range(NH):
        h = (2 * (1 - core) + i) % NH
        hs = pl.ds(pl.multiple_of(h * W, W), W)
        k, inv, kb, tk, tv, ttk, ttz, e0, f0, e1, f1 = local_maps(
            kraw_ref[:, hs], v_ref[:, hs], q_ref[:, hs], g_ref[:, hs], rate_base * rate_ref[h]
        )
        kf[h] = k
        invf[h] = jnp.broadcast_to(inv, (W, W))
        kbs[h] = kb
        tks[h] = tk
        tvs[h] = tv
        ttks[h] = ttk
        ttzs[h] = ttz
        maps[h, 0, :W] = e0
        maps[h, 0, W:] = f0
        maps[h, 1, :W] = e1
        maps[h, 1, W:] = f1
        if i == 0:
            pl.semaphore_wait(barrier, partners)
        if i < 2:
            seq_copy(maps.at[h], sib_maps.at[i], sm_ss, sm_rs, sib).start()

    sm_sum = seq_copy(sib_maps, sib_maps, sm_ss, sm_rs, sib)
    sm_sum.wait_recv()
    for i in range(2):
        h = 2 * core + i
        for role in range(2):
            here, there = maps[h, role], sib_maps[i, role]
            mine_first = core == role
            one = jnp.where(mine_first, here, there)
            first[i, role] = one
            chip_maps[i, role] = join(one, jnp.where(mine_first, there, here)).astype(bf16)
            slot = x if role == 0 else NX - 1 - x
            local = (x == h) & (core == role)

            @pl.when(jnp.logical_not(local))
            def _():
                seq_copy(
                    chip_maps.at[i, role], ef_recv.at[slot], ef_ss, ef_rs, dev(y, h, role)
                ).start()

            @pl.when(local)
            def _():
                ef_recv[slot] = chip_maps[i, role]

    zp = zme % 2
    half_rows = pl.ds(pl.multiple_of(zp * (W // 2), W // 2), W // 2)
    src_me = y * NC + core

    def tok_cols(yy, xx, cc):
        return pl.ds(pl.multiple_of(dev(yy, xx, cc) * W, W), W)

    def tok_start(yy, cc):
        for xx in range(NX):
            seq_copy(
                tok_ref.at[half_rows, tok_cols(yy, xx, cc)], tokcol.at[zp, src_me, xx],
                tok_ss, tok_rs, dev(yy, x, cc),
            ).start()

    for i in (2, 1, 3):
        for cc in range(NC):
            tok_start((y + i) % NY, cc)
    tok_start(y, 1 - core)
    for xx in range(NX):
        tokcol[zp, src_me, xx] = tok_ref[half_rows, tok_cols(y, xx, core)]
    tok_all = tokcol.at[0, pl.ds(0, 2 * NY - 1)]
    tok_sum = seq_copy(tok_all, tok_all, tok_ss, tok_rs, sib)
    tz_out = head_copy(tokcol.at[zp], tokcol.at[zp], tz_ss, tz_rs, zme + 1 - 2 * zp)
    tz_in = head_copy(tokcol.at[1 - zp], tokcol.at[1 - zp], tz_ss, tz_rs, zme + 1 - 2 * zp)

    def count(ref, ss, rs, act):
        few = ref.at[pl.ds(0, NX - 1)]

        @pl.when(hands)
        def _():
            act(seq_copy(few, few, ss, rs, sib))

        @pl.when(jnp.logical_not(hands))
        def _():
            act(seq_copy(ref, ref, ss, rs, sib))

    count(ef_recv, ef_ss, ef_rs, lambda c: c.wait_recv())
    for i in range(2):
        nodes[i] = join(ef_recv[2 * i], ef_recv[2 * i + 1])
    tot_send[...] = join(nodes[0], nodes[1]).astype(bf16)

    pos = jnp.where(core == 0, y, NY - 1 - y)
    for to_pos in range(NY - 1, 0, -1):
        to_y = jnp.where(core == 0, to_pos, NY - 1 - to_pos)

        @pl.when(to_pos > pos)
        def _():
            seq_copy(
                tot_send, tot_recv.at[pos], tot_ss.at[to_pos], tot_rs.at[pos],
                dev(to_y, x, core),
            ).start()

    tok_sum.wait_recv()
    tz_out.start()

    state[...] = jnp.where(core == 0, w0_ref[x].T, 0.0)
    for j in range(NY - 1):
        frm_y = jnp.where(core == 0, j, NY - 1 - j)

        @pl.when(j < pos)
        def _():
            seq_copy(
                tot_send, tot_recv.at[j], tot_ss.at[0], tot_rs.at[j], dev(frm_y, x, core)
            ).wait_recv()
            state[...] = apply(state[...], tot_recv[j])

    xs = [None] * NX
    xs[0] = state[...]
    xs[2] = apply(xs[0], nodes[0])
    xs[1] = apply(xs[0], ef_recv[0])
    xs[3] = apply(xs[2], ef_recv[2])
    spot = 2 * (x % 2) + core
    for slot in range(NX):
        x_send[slot] = xs[slot].astype(bf16)
        to = jnp.where(core == 0, slot, NX - 1 - slot)
        local = hands & (to == x)

        @pl.when(jnp.logical_not(local))
        def _():
            seq_copy(x_send.at[slot], x_in.at[spot], x_ss, x_rs, dev(y, to, x // 2)).start()

        @pl.when(local)
        def _():
            x_in[spot] = x_send[slot]

    count(x_in, x_ss, x_rs, lambda c: c.wait_recv())
    for i in range(2):
        for role in range(2):
            at_first = x_in[2 * i + role]
            at_second = apply(at_first.astype(f32), first[i, role]).astype(bf16)
            wl[2 * core + i, role] = jnp.where(core == role, at_first, at_second)
            x_sib[i, role] = jnp.where(core == role, at_second, at_first)
    own_two = wl.at[pl.ds(2 * core, 2)]
    other_two = wl.at[pl.ds(2 * (1 - core), 2)]
    x_out = seq_copy(x_sib, own_two, xs_ss, xs_rs, sib)
    x_out.start()

    below, above = dev((y + NY - 1) % NY, x, core), dev((y + 1) % NY, x, core)
    src_at = [((y + i) % NY) * NC + core for i in range(NY)]
    low, high = pl.ds(0, W // 2), pl.ds(W // 2, W // 2)

    def ag_copy(half, off, kind, to):
        ref = raw_all.at[half, src_at[off]]
        if kind >= 2:
            ref = raw_all.at[half, src_at[off], low if kind == 2 else high]
        return seq_copy(ref, ref, ag_ss.at[half], ag_rs.at[half, kind], to)

    def sib_copy(half, off, cc):
        ref = raw_all.at[half, ((y + off) % NY) * NC + cc]
        return seq_copy(ref, ref, ag_ss.at[half], sib_rs.at[half, off], sib)

    rates = [rate_base * rate_ref[h] for h in range(NH)]
    raws = []
    for half in range(2):
        @pl.when(core != half)
        def _():
            seq_copy(other_two, other_two, xs_ss, xs_rs, sib).wait_recv()

        for h in (2 * half, 2 * half + 1):
            hs = slice(h * W, h * W + W)
            bi, bj = batch_of()
            r = rates[h]
            w, l = wl[h, 0], wl[h, 1]
            q, g, kb = q_ref[:, hs], g_ref[:, hs], kbs[h]
            ub = (nt(tks[h], w) - tvs[h]).astype(bf16)
            yy = nt(ttks[h], l) + ttzs[h]
            yb = yy.astype(bf16)
            gv_ref[:, hs] = (r * yy).astype(bf16)
            ubs[h] = ub
            pm = jnp.where(bi <= bj, nt(ub, g), 0.0).astype(bf16)
            sm = (
                jnp.where(bi < bj, nt(ub, yb), 0.0) + jnp.where(bi > bj, nt(yb, ub), 0.0)
            ).astype(bf16)
            ka = -r * (mm(ub, l) + mm(yb, w) + mm(pm, q) - r * mm(sm, kb))
            k = kf[h]
            along = jnp.sum(k * ka, axis=1, keepdims=True)
            raws.append(((ka - k * along) * invf[h]).astype(bf16))
        raw_all[half, src_me] = jnp.concatenate(raws[-2:], axis=1)
        ag_copy(half, 0, 0, above).start()
        ag_copy(half, 0, 1, below).start()
        sib_copy(half, 0, core).start()

    raw = jnp.concatenate([raw_all[0, src_me], raw_all[1, src_me]], axis=1)

    def part(off):
        rows = pl.ds(pl.multiple_of(z_at[off] * NH * W, NH * W), NH * W)
        out = nt(raw, kw_ref[rows, :])
        zs[off, 0] = out[:, :2 * W].astype(bf16)
        zs[off, 1] = out[:, 2 * W:].astype(bf16)

    def z_copy(way, n, half):
        off = 4 - n if way == 0 else (4 + n) % NZ
        to = (2 if n == 0 else 1) if way == 0 else (6 if n == 0 else 7)
        return head_copy(
            zs.at[off, half], zr.at[way, n, half], z_ss, z_rs.at[way, 2 * n + half], z_at[to]
        )

    def z_add(way, n, half):
        off = 4 - n if way == 0 else (4 + n) % NZ
        z_copy(way, n - 1, half).wait_recv()
        total = zs[off, half].astype(f32) + zr[way, n - 1, half].astype(f32)
        if n == 2 and half == way:
            z_copy(way, 0, half).wait_recv()
            total = total + zr[way, 0, half].astype(f32)
        zs[off, half] = total.astype(bf16)
        z_copy(way, n, half).start()

    part(3)
    z_copy(0, 1, 1).start()
    z_copy(0, 1, 0).start()
    part(5)
    z_copy(1, 1, 0).start()
    z_copy(1, 1, 1).start()
    part(4)
    z_copy(0, 0, 0).start()
    z_copy(1, 0, 1).start()
    part(2)
    part(6)

    def relay(half):
        ag_copy(half, 3, 0, sib).wait_recv()
        ag_copy(half, 3, 2, above).start()
        sib_copy(half, 3, core).start()
        ag_copy(half, 1, 1, sib).wait_recv()
        ag_copy(half, 1, 3, below).start()
        sib_copy(half, 1, core).start()

    def far(half):
        ag_copy(half, 2, 2, sib).wait_recv()
        ag_copy(half, 2, 3, sib).wait_recv()
        sib_copy(half, 2, core).start()

    relay(0)
    relay(1)
    z_add(0, 2, 1)
    z_add(1, 2, 0)
    z_add(0, 2, 0)
    z_add(1, 2, 1)

    tz_in.wait_recv()

    def turn(src, c):
        cols = pl.ds(pl.multiple_of(src * W, W), W)
        for xx in range(NX):
            both = jnp.concatenate([tokcol[0, src, xx], tokcol[1, src, xx]], axis=0)
            tok_t[xx * W:xx * W + W, cols] = both.T
        return c

    lax.fori_loop(0, NC * NY, turn, 0)
    part(1)
    part(7)
    far(0)
    z_add(0, 3, 1)
    z_add(1, 3, 0)

    x_at = [(x + i) % NX for i in range(NX)]
    right, left = dev(y, x_at[1], core), dev(y, x_at[3], core)

    def rs_copy(half, off, piece):
        rows = low if piece == 0 else high
        to_right = off == 1 or (off == 2 and piece == 0)
        return seq_copy(
            rs_s.at[half, off, rows], rs_r.at[half, off, rows], rs_ss.at[half],
            rs_rs.at[half, 2 * off + piece], right if to_right else left,
        )

    def products(half):
        for off in range(NY):
            sib_copy(half, off, 1 - core).wait_recv()
        out = mm(tok_t[...], raw_all[half].reshape(NC * NY * W, 2 * W))
        for xx in range(NX):
            psum[half, xx] = out[xx * W:xx * W + W]
        for off in (2, 1, 3):
            rs_s[half, off] = psum[half, x_at[off]].astype(bf16)
            if off == 2:
                rs_copy(half, 2, 0).start()
                rs_copy(half, 2, 1).start()
            else:
                rs_copy(half, off, 1 if off == 1 else 0).start()

    def rs_add(half):
        for off, piece in ((1, 0), (3, 1)):
            rows = slice(0, W // 2) if piece == 0 else slice(W // 2, W)
            rs_copy(half, 2, piece).wait_recv()
            rs_s[half, off, rows] = (
                psum[half, x_at[off], rows] + rs_r[half, 2, rows].astype(f32)
            ).astype(bf16)
            rs_copy(half, off, piece).start()

    def rs_end(half):
        for off in (1, 3):
            for piece in range(2):
                rs_copy(half, off, piece).wait_recv()
        gkw_ref[:, 2 * W * half:2 * W * (half + 1)] = (
            psum[half, x] + rs_r[half, 1].astype(f32) + rs_r[half, 3].astype(f32)
        )

    products(0)
    z_add(0, 3, 0)
    z_add(1, 3, 1)
    far(1)
    products(1)
    part(0)

    def grad_query(h):
        hs = slice(h * W, h * W + W)
        bi, bj = batch_of()
        g = g_ref[:, hs]
        lower = jnp.where(bi >= bj, nt(g, ubs[h]), 0.0).astype(bf16)
        gq_ref[:, hs] = (mm(g, wl[h, 0]) - rates[h] * mm(lower, kbs[h])).astype(bf16)

    grad_query(0)
    grad_query(1)
    rs_add(0)
    grad_query(2)
    grad_query(3)
    rs_add(1)

    for half in range(2):
        z_copy(0, 3, half).wait_recv()
        z_copy(1, 3, half).wait_recv()
        gt_ref[:, 2 * W * half:2 * W * (half + 1)] = (
            zs[0, half].astype(f32) + zr[0, 3, half].astype(f32) + zr[1, 3, half].astype(f32)
        ).astype(bf16)
    rs_end(0)
    rs_end(1)

    sm_sum.wait_send()
    count(ef_recv, ef_ss, ef_rs, lambda c: c.wait_send())
    tok_sum.wait_send()
    tz_out.wait_send()
    for to_pos in range(1, NY):
        @pl.when(to_pos > pos)
        def _():
            seq_copy(tot_send, tot_recv.at[0], tot_ss.at[to_pos], tot_rs.at[0], sib).wait_send()
    count(x_in, x_ss, x_rs, lambda c: c.wait_send())
    x_out.wait_send()
    for half in range(2):
        ref = raw_all.at[half, pl.ds(0, 7)]
        seq_copy(ref, ref, ag_ss.at[half], sib_rs.at[half, 0], sib).wait_send()
        ref = rs_s.at[half, pl.ds(0, 3)]
        seq_copy(ref, ref, rs_ss.at[half], rs_rs.at[half, 0], sib).wait_send()
    some_z = zs.at[pl.ds(0, 7)]
    head_copy(some_z, some_z, z_ss, z_rs.at[0, 0], z_at[1]).wait_send()


def hand_over(a0, a1, a2, a3, b0, b1, b2, b3):
    for a, b in ((a0, b0), (a1, b1), (a2, b2), (a3, b3)):
        b[...] = a[...]


def per_device(tokens, key_weight, queries, values, grad_out, inner_start, head_rate):
    vmem = pl.BlockSpec(memory_space=pltpu.VMEM)
    smem = pl.BlockSpec(memory_space=pltpu.SMEM)
    anywhere = pl.BlockSpec(memory_space=pl.ANY)
    cols = NH * W
    sem = pltpu.SemaphoreType.DMA
    shapes = (
        jax.ShapeDtypeStruct((W, cols), bf16),
        jax.ShapeDtypeStruct((W, cols), f32),
        jax.ShapeDtypeStruct((W, cols), bf16),
        jax.ShapeDtypeStruct((W, cols), bf16),
    )
    outs = pl.pallas_call(
        kernel,
        out_shape=shapes,
        in_specs=[anywhere] * 6 + [smem],
        out_specs=(vmem,) * 4,
        scratch_shapes=[
            pltpu.VMEM(tokens.shape, bf16),
            pltpu.VMEM(key_weight.shape, bf16),
            pltpu.VMEM((W, cols), bf16),
            pltpu.VMEM((W, cols), bf16),
            pltpu.VMEM((W, cols), bf16),
            pltpu.VMEM((NH, W, W), f32),
            pltpu.VMEM((W, cols), f32),
            pltpu.VMEM((2, NC * NY, NX, W // 2, W), bf16),
            pltpu.VMEM((NX * W, NC * NY * W), bf16),
            pltpu.VMEM((NH, 2, 2 * W, W), bf16),
            pltpu.VMEM((2, 2, 2 * W, W), bf16),
            pltpu.VMEM((2, 2, 2 * W, W), bf16),
            pltpu.VMEM((2, 2, 2 * W, W), bf16),
            pltpu.VMEM((NX, 2 * W, W), bf16),
            pltpu.VMEM((2 * W, W), bf16),
            pltpu.VMEM((NY, 2 * W, W), bf16),
            pltpu.VMEM((2, 2 * W, W), f32),
            pltpu.VMEM((W, W), f32),
            pltpu.VMEM((NX, W, W), bf16),
            pltpu.VMEM((4, W, W), bf16),
            pltpu.VMEM((2, 2, W, W), bf16),
            pltpu.VMEM((NH, 2, W, W), bf16),
            pltpu.VMEM((NH, W, W), f32),
            pltpu.VMEM((NH, W, W), f32),
            pltpu.VMEM((NH, W, W), bf16),
            pltpu.VMEM((NH, W, W), bf16),
            pltpu.VMEM((NH, W, W), f32),
            pltpu.VMEM((NH, W, W), bf16),
            pltpu.VMEM((NH, W, W), f32),
            pltpu.VMEM((NH, W, W), bf16),
            pltpu.VMEM((2, NC * NY, W, 2 * W), bf16),
            pltpu.VMEM((2, NX, W, 2 * W), f32),
            pltpu.VMEM((2, NX, W, 2 * W), bf16),
            pltpu.VMEM((2, NX, W, 2 * W), bf16),
            pltpu.VMEM((NZ, 2, W, 2 * W), bf16),
            pltpu.VMEM((2, 4, 2, W, 2 * W), bf16),
            sem((5 + KW_PARTS,)),
            sem, sem, sem, sem,
            sem, sem, sem, sem,
            sem((NY,)), sem((NY,)),
            sem, sem, sem, sem,
            sem((2,)), sem((2, 4)), sem((2, 4)),
            sem((2,)), sem((2, 8)),
            sem, sem((2, 8)),
        ],
        compiler_params=pltpu.CompilerParams(
            collective_id=0, has_side_effects=True, vmem_limit_bytes=56 * 1024 * 1024
        ),
        name="layer",
    )(tokens, key_weight, queries, values, grad_out, inner_start, head_rate)
    return pl.pallas_call(
        hand_over,
        out_shape=shapes,
        in_specs=[vmem] * 4,
        out_specs=(vmem,) * 4,
        name="hand_over",
    )(*outs)


def solution(mesh):
    placed = (
        P("seq", None),
        P(None, "head"),
        P("seq", "head"),
        P("seq", "head"),
        P("seq", "head"),
        P("head", None, None),
        P("head"),
    )
    return jax.shard_map(
        per_device,
        mesh=mesh,
        in_specs=placed,
        out_specs=(P("seq", "head"),) * 4,
        check_vma=False,
    )
```

time: 64.7 us -> 59.3 us (0.917)
  Pallas kernels: 63.9 us -> 58.6 us
    pallas_call x1, Pallas kernels: 62 us -> 56.6 us  [per_device(): pl.pallas_call(kernel, out_shape=shapes, in_specs=[anywhere] * 6 + [smem]...]
where the time goes in v3:
time: 59.3 us; the launch traced here: 59.2 us
  Pallas kernels  58.6 us (99%)
  between operations  0.64 us (1%)
    pallas_call x1, Pallas kernels, per_device(): pl.pallas_call(kernel, out_shape=shapes, in_specs=[anywhere] * 6 + [smem]...  56.6 us
    pallas_call x1, Pallas kernels, per_device(): pl.pallas_call(hand_over, out_shape=shapes, in_specs=[vmem] * 4, out_spec...  1.96 us

profile of v3, /device:TPU:1, one launch (start us, length us, event | category | flops | bytes accessed | tf_op | source)
XLA Modules:
  0.0 59.2 jit_solution(7276444395123912076)
XLA Ops:
  0.6 56.6 %layer.1 = (bf16[128,512]{1,0:T(8,128)(2,1)}, f32[128,512]{1,0:T(8,128)}, bf16[128,512]{1,0:T(8,128)(2,1)}, bf16[128,512]{1,0:T(8,128)(2,1)}) custom-call(bf16[128,4096]{1,0:T(8,128)(2,1)} %tok_hbm.1, bf16[4096,512]{1,0:T(8,128)(2,1)} %kw_hbm.1, bf16[128,512]{1,0:T(8,128)(2,1)} %q_hbm.1, bf16[128,512]{1,0:T(8,128)(2,1)} %v_hbm.1, bf16[128,512]{1,0:T(8,128)(2,1)} %g_hbm.1, ...), custom_call_target="tpu_custom_call" | custom-call | tf_op jit(solution)/shard_map/layer/pallas_call | solution.py:517
  57.3 2.0 %hand_over.1 = (bf16[128,512]{1,0:T(8,128)(2,1)}, f32[128,512]{1,0:T(8,128)}, bf16[128,512]{1,0:T(8,128)(2,1)}, bf16[128,512]{1,0:T(8,128)(2,1)}) custom-call(bf16[128,512]{1,0:T(8,128)(2,1)} %get-tuple-element.8.a0, f32[128,512]{1,0:T(8,128)} %get-tuple-element.9.a1, bf16[128,512]{1,0:T(8,128)(2,1)} %get-tuple-element.10.a2, ...), custom_call_target="tpu_custom_call" | custom-call | tf_op jit(solution)/shard_map/hand_over/pallas_call | solution.py:573

commit v4 on v3

--- a/solution.py
+++ b/solution.py
@@ -36,33 +36,58 @@
     return rows, cols
 
 
-def local_maps(kraw, v, q, g, r):
+def local_maps(kraws, vs, qs, gs, rs):
+    n = range(len(rs))
     bi, bj = batch_of()
-    inv = lax.rsqrt(jnp.sum(kraw * kraw, axis=1, keepdims=True) + norm_eps)
-    k = kraw * inv
-    kb = k.astype(bf16)
-    m = r * nt(kb, kb)
-    x1 = jnp.where(((bi >> 1) == (bj >> 1)) & (bi > bj), m, 0.0)
-    x2 = jnp.where(((bi >> 2) == (bj >> 2)) & ((bi >> 1) > (bj >> 1)), m, 0.0)
-    x3 = jnp.where((bi >> 2) > (bj >> 2), m, 0.0)
     rows = lax.broadcasted_iota(jnp.int32, (W, W), 0)
     cols = lax.broadcasted_iota(jnp.int32, (W, W), 1)
-    t1 = jnp.where(rows == cols, 1.0, 0.0) - x1
-    t1b = t1.astype(bf16)
-    t2 = t1 - mm(mm(t1b, x2.astype(bf16)).astype(bf16), t1b)
-    t2b = t2.astype(bf16)
-    t3 = t2 - mm(mm(t2b, x3.astype(bf16)).astype(bf16), t2b)
-    tb = t3.astype(bf16)
-    tk = mm(tb, kb).astype(bf16)
-    tv = mm(tb, v)
-    z = mm(jnp.where(bi <= bj, nt(kb, q), 0.0).astype(bf16), g).astype(bf16)
-    ttk = tn(tb, kb).astype(bf16)
-    ttz = tn(tb, z)
-    e0 = (-r * tn(tk, kb)).astype(bf16)
-    f0 = (r * tn(tv.astype(bf16), kb)).astype(bf16)
-    e1 = (-r * tn(kb, tk)).astype(bf16)
-    f1 = (tn(g, q) - r * tn(ttz.astype(bf16), kb)).astype(bf16)
-    return k, inv, kb, tk, tv, ttk, ttz, e0, f0, e1, f1
+    eye = jnp.where(rows == cols, 1.0, 0.0)
+    near = ((bi >> 1) == (bj >> 1)) & (bi > bj)
+    middle = ((bi >> 2) == (bj >> 2)) & ((bi >> 1) > (bj >> 1))
+    distant = (bi >> 2) > (bj >> 2)
+    invs = [lax.rsqrt(jnp.sum(kr * kr, axis=1, keepdims=True) + norm_eps) for kr in kraws]
+    ks = [kraws[i] * invs[i] for i in n]
+    kbs = [k.astype(bf16) for k in ks]
+    ms = [rs[i] * nt(kbs[i], kbs[i]) for i in n]
+    zs = [jnp.where(bi <= bj, nt(kbs[i], qs[i]), 0.0).astype(bf16) for i in n]
+    ts = [eye - jnp.where(near, m, 0.0) for m in ms]
+    for mask in (middle, distant):
+        tbs = [t.astype(bf16) for t in ts]
+        us = [mm(tbs[i], jnp.where(mask, ms[i], 0.0).astype(bf16)).astype(bf16) for i in n]
+        ts = [ts[i] - mm(us[i], tbs[i]) for i in n]
+    zs = [mm(zs[i], gs[i]).astype(bf16) for i in n]
+    qgs = [tn(gs[i], qs[i]) for i in n]
+    tbs = [t.astype(bf16) for t in ts]
+    tks = [mm(tbs[i], kbs[i]).astype(bf16) for i in n]
+    tvs = [mm(tbs[i], vs[i]) for i in n]
+    ttzs = [tn(tbs[i], zs[i]) for i in n]
+    ttks = [tn(tbs[i], kbs[i]).astype(bf16) for i in n]
+    e0s = [(-rs[i] * tn(tks[i], kbs[i])).astype(bf16) for i in n]
+    e1s = [(-rs[i] * tn(kbs[i], tks[i])).astype(bf16) for i in n]
+    f0s = [(rs[i] * tn(tvs[i].astype(bf16), kbs[i])).astype(bf16) for i in n]
+    f1s = [(qgs[i] - rs[i] * tn(ttzs[i].astype(bf16), kbs[i])).astype(bf16) for i in n]
+    return ks, invs, kbs, tks, tvs, ttks, ttzs, e0s, f0s, e1s, f1s
+
+
+def final_rows(k, inv, kb, tk, tv, ttk, ttz, v, q, g, r, w, l):
+    n = range(len(r))
+    bi, bj = batch_of()
+    ubs = [(nt(tk[i], w[i]) - tv[i]).astype(bf16) for i in n]
+    ys = [nt(ttk[i], l[i]) + ttz[i] for i in n]
+    ybs = [y.astype(bf16) for y in ys]
+    pms = [jnp.where(bi <= bj, nt(ubs[i], g[i]), 0.0).astype(bf16) for i in n]
+    sms = [
+        jnp.where(
+            bi < bj, nt(ubs[i], ybs[i]), jnp.where(bi > bj, nt(ybs[i], ubs[i]), 0.0)
+        ).astype(bf16)
+        for i in n
+    ]
+    kas = [mm(ubs[i], l[i]) + mm(ybs[i], w[i]) for i in n]
+    kas = [kas[i] + mm(pms[i], q[i]) for i in n]
+    kas = [-r[i] * (kas[i] - r[i] * mm(sms[i], kb[i])) for i in n]
+    alongs = [jnp.sum(k[i] * kas[i], axis=1, keepdims=True) for i in n]
+    raws = [((kas[i] - k[i] * alongs[i]) * inv[i]).astype(bf16) for i in n]
+    return ubs, [(r[i] * ys[i]).astype(bf16) for i in n], raws
 
 
 def join(a, b):
@@ -146,31 +171,63 @@
     kraw_ref[...] = kraw
     for load in loads[1 + KW_PARTS:]:
         load.wait()
-    for i in range(NH):
-        h = (2 * (1 - core) + i) % NH
-        hs = pl.ds(pl.multiple_of(h * W, W), W)
-        k, inv, kb, tk, tv, ttk, ttz, e0, f0, e1, f1 = local_maps(
-            kraw_ref[:, hs], v_ref[:, hs], q_ref[:, hs], g_ref[:, hs], rate_base * rate_ref[h]
-        )
-        kf[h] = k
-        invf[h] = jnp.broadcast_to(inv, (W, W))
-        kbs[h] = kb
-        tks[h] = tk
-        tvs[h] = tv
-        ttks[h] = ttk
-        ttzs[h] = ttz
-        maps[h, 0, :W] = e0
-        maps[h, 0, W:] = f0
-        maps[h, 1, :W] = e1
-        maps[h, 1, W:] = f1
-        if i == 0:
-            pl.semaphore_wait(barrier, partners)
-        if i < 2:
-            seq_copy(maps.at[h], sib_maps.at[i], sm_ss, sm_rs, sib).start()
+    zp = zme % 2
+    half_rows = pl.ds(pl.multiple_of(zp * (W // 2), W // 2), W // 2)
+    src_me = y * NC + core
+
+    def tok_cols(yy, xx, cc):
+        return pl.ds(pl.multiple_of(dev(yy, xx, cc) * W, W), W)
+
+    def tok_start(yy, cc):
+        for xx in range(NX):
+            seq_copy(
+                tok_ref.at[half_rows, tok_cols(yy, xx, cc)], tokcol.at[zp, src_me, xx],
+                tok_ss, tok_rs, dev(yy, x, cc),
+            ).start()
+
+    sm_out = seq_copy(maps.at[pl.ds(2 * (1 - core), 2)], sib_maps, sm_ss, sm_rs, sib)
+    pl.semaphore_wait(barrier, partners)
+    for cc in range(NC):
+        tok_start((y + 2) % NY, cc)
+    tok_start((y + 1) % NY, core)
+    tok_start((y + 1) % NY, 1 - core)
+    for cc in range(NC):
+        tok_start((y + 3) % NY, cc)
+    tok_start(y, 1 - core)
+    for pair in range(2):
+        base = 2 * ((1 - core + pair) % 2)
+        cut = pl.ds(pl.multiple_of(base * W, 2 * W), 2 * W)
+
+        def two(ref):
+            both = ref[:, cut]
+            return [both[:, :W], both[:, W:]]
+
+        found = local_maps(
+            two(kraw_ref), two(v_ref), two(q_ref), two(g_ref),
+            [rate_base * rate_ref[base + i] for i in range(2)],
+        )
+        for i in range(2):
+            h = base + i
+            k, inv, kb, tk, tv, ttk, ttz, e0, f0, e1, f1 = [each[i] for each in found]
+            maps[h, 0, :W] = e0
+            maps[h, 0, W:] = f0
+            maps[h, 1, :W] = e1
+            maps[h, 1, W:] = f1
+            kf[h] = k
+            invf[h] = jnp.broadcast_to(inv, (W, W))
+            kbs[h] = kb
+            tks[h] = tk
+            tvs[h] = tv
+            ttks[h] = ttk
+            ttzs[h] = ttz
+        if pair == 0:
+            sm_out.start()
 
     sm_sum = seq_copy(sib_maps, sib_maps, sm_ss, sm_rs, sib)
     sm_sum.wait_recv()
-    for i in range(2):
+    i_far = jnp.where(hands, 1 - x % 2, x % 2)
+    for step in range(2):
+        i = i_far if step == 0 else 1 - i_far
         h = 2 * core + i
         for role in range(2):
             here, there = maps[h, role], sib_maps[i, role]
@@ -191,24 +248,6 @@
             def _():
                 ef_recv[slot] = chip_maps[i, role]
 
-    zp = zme % 2
-    half_rows = pl.ds(pl.multiple_of(zp * (W // 2), W // 2), W // 2)
-    src_me = y * NC + core
-
-    def tok_cols(yy, xx, cc):
-        return pl.ds(pl.multiple_of(dev(yy, xx, cc) * W, W), W)
-
-    def tok_start(yy, cc):
-        for xx in range(NX):
-            seq_copy(
-                tok_ref.at[half_rows, tok_cols(yy, xx, cc)], tokcol.at[zp, src_me, xx],
-                tok_ss, tok_rs, dev(yy, x, cc),
-            ).start()
-
-    for i in (2, 1, 3):
-        for cc in range(NC):
-            tok_start((y + i) % NY, cc)
-    tok_start(y, 1 - core)
     for xx in range(NX):
         tokcol[zp, src_me, xx] = tok_ref[half_rows, tok_cols(y, xx, core)]
     tok_all = tokcol.at[0, pl.ds(0, 2 * NY - 1)]
@@ -303,35 +342,29 @@
         return seq_copy(ref, ref, ag_ss.at[half], sib_rs.at[half, off], sib)
 
     rates = [rate_base * rate_ref[h] for h in range(NH)]
-    raws = []
-    for half in range(2):
-        @pl.when(core != half)
-        def _():
+    for pair in range(2):
+        half = (core + pair) % 2
+        if pair == 1:
             seq_copy(other_two, other_two, xs_ss, xs_rs, sib).wait_recv()
-
-        for h in (2 * half, 2 * half + 1):
-            hs = slice(h * W, h * W + W)
-            bi, bj = batch_of()
-            r = rates[h]
-            w, l = wl[h, 0], wl[h, 1]
-            q, g, kb = q_ref[:, hs], g_ref[:, hs], kbs[h]
-            ub = (nt(tks[h], w) - tvs[h]).astype(bf16)
-            yy = nt(ttks[h], l) + ttzs[h]
-            yb = yy.astype(bf16)
-            gv_ref[:, hs] = (r * yy).astype(bf16)
-            ubs[h] = ub
-            pm = jnp.where(bi <= bj, nt(ub, g), 0.0).astype(bf16)
-            sm = (
-                jnp.where(bi < bj, nt(ub, yb), 0.0) + jnp.where(bi > bj, nt(yb, ub), 0.0)
-            ).astype(bf16)
-            ka = -r * (mm(ub, l) + mm(yb, w) + mm(pm, q) - r * mm(sm, kb))
-            k = kf[h]
-            along = jnp.sum(k * ka, axis=1, keepdims=True)
-            raws.append(((ka - k * along) * invf[h]).astype(bf16))
-        raw_all[half, src_me] = jnp.concatenate(raws[-2:], axis=1)
+        hs = [2 * half, 2 * half + 1]
+        cut = pl.ds(pl.multiple_of(half * 2 * W, 2 * W), 2 * W)
+
+        def two(ref):
+            both = ref[:, cut]
+            return [both[:, :W], both[:, W:]]
+
+        kept = [[ref[h] for h in hs] for ref in (kf, invf, kbs, tks, tvs, ttks, ttzs)]
+        us, gvs, raws = final_rows(
+            *kept, None, two(q_ref), two(g_ref),
+            [rate_base * rate_ref[h] for h in hs], [wl[h, 0] for h in hs], [wl[h, 1] for h in hs],
+        )
+        raw_all[half, src_me] = jnp.concatenate(raws, axis=1)
         ag_copy(half, 0, 0, above).start()
         ag_copy(half, 0, 1, below).start()
         sib_copy(half, 0, core).start()
+        gv_ref[:, cut] = jnp.concatenate(gvs, axis=1)
+        for i in range(2):
+            ubs[hs[i]] = us[i]
 
     raw = jnp.concatenate([raw_all[0, src_me], raw_all[1, src_me]], axis=1)
 
@@ -358,18 +391,6 @@
         zs[off, half] = total.astype(bf16)
         z_copy(way, n, half).start()
 
-    part(3)
-    z_copy(0, 1, 1).start()
-    z_copy(0, 1, 0).start()
-    part(5)
-    z_copy(1, 1, 0).start()
-    z_copy(1, 1, 1).start()
-    part(4)
-    z_copy(0, 0, 0).start()
-    z_copy(1, 0, 1).start()
-    part(2)
-    part(6)
-
     def relay(half):
         ag_copy(half, 3, 0, sib).wait_recv()
         ag_copy(half, 3, 2, above).start()
@@ -383,28 +404,12 @@
         ag_copy(half, 2, 3, sib).wait_recv()
         sib_copy(half, 2, core).start()
 
-    relay(0)
-    relay(1)
-    z_add(0, 2, 1)
-    z_add(1, 2, 0)
-    z_add(0, 2, 0)
-    z_add(1, 2, 1)
-
-    tz_in.wait_recv()
-
     def turn(src, c):
         cols = pl.ds(pl.multiple_of(src * W, W), W)
         for xx in range(NX):
             both = jnp.concatenate([tokcol[0, src, xx], tokcol[1, src, xx]], axis=0)
             tok_t[xx * W:xx * W + W, cols] = both.T
         return c
-
-    lax.fori_loop(0, NC * NY, turn, 0)
-    part(1)
-    part(7)
-    far(0)
-    z_add(0, 3, 1)
-    z_add(1, 3, 0)
 
     x_at = [(x + i) % NX for i in range(NX)]
     right, left = dev(y, x_at[1], core), dev(y, x_at[3], core)
@@ -448,13 +453,6 @@
             psum[half, x] + rs_r[half, 1].astype(f32) + rs_r[half, 3].astype(f32)
         )
 
-    products(0)
-    z_add(0, 3, 0)
-    z_add(1, 3, 1)
-    far(1)
-    products(1)
-    part(0)
-
     def grad_query(h):
         hs = slice(h * W, h * W + W)
         bi, bj = batch_of()
@@ -462,12 +460,40 @@
         lower = jnp.where(bi >= bj, nt(g, ubs[h]), 0.0).astype(bf16)
         gq_ref[:, hs] = (mm(g, wl[h, 0]) - rates[h] * mm(lower, kbs[h])).astype(bf16)
 
-    grad_query(0)
-    grad_query(1)
+    part(3)
+    z_copy(0, 1, 1).start()
+    z_copy(0, 1, 0).start()
+    part(5)
+    z_copy(1, 1, 0).start()
+    z_copy(1, 1, 1).start()
+    part(4)
+    z_copy(0, 0, 0).start()
+    z_copy(1, 0, 1).start()
+    part(2)
+    part(6)
+    relay(core)
+    relay(1 - core)
+    z_add(0, 2, 1)
+    z_add(1, 2, 0)
+    tz_in.wait_recv()
+    lax.fori_loop(0, NC * NY, turn, 0)
+    far(core)
+    far(1 - core)
+    z_add(0, 2, 0)
+    z_add(1, 2, 1)
+    part(1)
+    part(7)
+    products(0)
+    products(1)
+    z_add(0, 3, 1)
+    z_add(1, 3, 0)
+    part(0)
     rs_add(0)
-    grad_query(2)
-    grad_query(3)
     rs_add(1)
+    z_add(0, 3, 0)
+    z_add(1, 3, 1)
+    for h in range(NH):
+        grad_query(h)
 
     for half in range(2):
         z_copy(0, 3, half).wait_recv()

time: 59.3 us -> 51.1 us (0.86)
  Pallas kernels: 58.6 us -> 50.3 us
    pallas_call x1, Pallas kernels: 56.6 us -> 48.3 us  [per_device(): pl.pallas_call(kernel, out_shape=shapes, in_specs=[anywhere] * 6 + [smem]...]
where the time goes in v4:
time: 51.1 us; the launch traced here: 50.9 us
  Pallas kernels  50.3 us (98%)
  between operations  0.64 us (1%)
    pallas_call x1, Pallas kernels, per_device(): pl.pallas_call(kernel, out_shape=shapes, in_specs=[anywhere] * 6 + [smem]...  48.3 us
    pallas_call x1, Pallas kernels, per_device(): pl.pallas_call(hand_over, out_shape=shapes, in_specs=[vmem] * 4, out_spec...  1.96 us

profile of v4, /device:TPU:1, one launch (start us, length us, event | category | flops | bytes accessed | tf_op | source)
XLA Modules:
  0.0 50.9 jit_solution(12271612990383319009)
XLA Ops:
  0.6 48.3 %layer.1 = (bf16[128,512]{1,0:T(8,128)(2,1)}, f32[128,512]{1,0:T(8,128)}, bf16[128,512]{1,0:T(8,128)(2,1)}, bf16[128,512]{1,0:T(8,128)(2,1)}) custom-call(bf16[128,4096]{1,0:T(8,128)(2,1)} %tok_hbm.1, bf16[4096,512]{1,0:T(8,128)(2,1)} %kw_hbm.1, bf16[128,512]{1,0:T(8,128)(2,1)} %q_hbm.1, bf16[128,512]{1,0:T(8,128)(2,1)} %v_hbm.1, bf16[128,512]{1,0:T(8,128)(2,1)} %g_hbm.1, ...), custom_call_target="tpu_custom_call" | custom-call | tf_op jit(solution)/shard_map/layer/pallas_call | solution.py:543
  49.0 2.0 %hand_over.1 = (bf16[128,512]{1,0:T(8,128)(2,1)}, f32[128,512]{1,0:T(8,128)}, bf16[128,512]{1,0:T(8,128)(2,1)}, bf16[128,512]{1,0:T(8,128)(2,1)}) custom-call(bf16[128,512]{1,0:T(8,128)(2,1)} %get-tuple-element.8.a0, f32[128,512]{1,0:T(8,128)} %get-tuple-element.9.a1, bf16[128,512]{1,0:T(8,128)(2,1)} %get-tuple-element.10.a2, ...), custom_call_target="tpu_custom_call" | custom-call | tf_op jit(solution)/shard_map/hand_over/pallas_call | solution.py:599

commit v5 on v4

--- a/solution.py
+++ b/solution.py
@@ -100,12 +100,12 @@
 
 def kernel(
     tok_hbm, kw_hbm, q_hbm, v_hbm, g_hbm, w0_hbm, rate_ref,
-    gt_ref, gkw_ref, gq_ref, gv_ref,
-    tok_ref, kw_ref, q_ref, v_ref, g_ref, w0_ref, kraw_ref,
+    gt_out, gkw_out, gq_out, gv_out,
+    gt_ref, gkw_ref, gq_ref, gv_ref, tok_ref, kw_ref, q_ref, v_ref, g_ref, w0_ref, kraw_ref,
     tokcol, tok_t, maps, sib_maps, first, chip_maps, ef_recv, tot_send, tot_recv, nodes,
     state, x_send, x_in, x_sib, wl,
     kf, invf, kbs, tks, tvs, ttks, ttzs, ubs, raw_all, psum, rs_s, rs_r, zs, zr,
-    in_s, tok_ss, tok_rs, tz_ss, tz_rs, sm_ss, sm_rs, ef_ss, ef_rs, tot_ss, tot_rs,
+    in_s, out_s, tok_ss, tok_rs, tz_ss, tz_rs, sm_ss, sm_rs, ef_ss, ef_rs, tot_ss, tot_rs,
     x_ss, x_rs, xs_ss, xs_rs, ag_ss, ag_rs, sib_rs, rs_ss, rs_rs, z_ss, z_rs,
 ):
     me = lax.axis_index("seq")
@@ -143,6 +143,13 @@
         loads.append(pltpu.make_async_copy(src, dst, in_s.at[1 + KW_PARTS + i]))
     for load in loads:
         load.start()
+
+    leave = [
+        pltpu.make_async_copy(src, dst, out_s.at[i])
+        for i, (src, dst) in enumerate(
+            ((gt_ref, gt_out), (gkw_ref, gkw_out), (gq_ref, gq_out), (gv_ref, gv_out))
+        )
+    ]
 
     barrier = pltpu.get_barrier_semaphore()
 
@@ -332,9 +339,8 @@
     low, high = pl.ds(0, W // 2), pl.ds(W // 2, W // 2)
 
     def ag_copy(half, off, kind, to):
-        ref = raw_all.at[half, src_at[off]]
-        if kind >= 2:
-            ref = raw_all.at[half, src_at[off], low if kind == 2 else high]
+        rows = low if kind in (0, 2, 5) else high
+        ref = raw_all.at[half, src_at[off], rows]
         return seq_copy(ref, ref, ag_ss.at[half], ag_rs.at[half, kind], to)
 
     def sib_copy(half, off, cc):
@@ -361,6 +367,8 @@
         raw_all[half, src_me] = jnp.concatenate(raws, axis=1)
         ag_copy(half, 0, 0, above).start()
         ag_copy(half, 0, 1, below).start()
+        ag_copy(half, 0, 4, above).start()
+        ag_copy(half, 0, 5, below).start()
         sib_copy(half, 0, core).start()
         gv_ref[:, cut] = jnp.concatenate(gvs, axis=1)
         for i in range(2):
@@ -371,32 +379,46 @@
     def part(off):
         rows = pl.ds(pl.multiple_of(z_at[off] * NH * W, NH * W), NH * W)
         out = nt(raw, kw_ref[rows, :])
-        zs[off, 0] = out[:, :2 * W].astype(bf16)
-        zs[off, 1] = out[:, 2 * W:].astype(bf16)
-
-    def z_copy(way, n, half):
-        off = 4 - n if way == 0 else (4 + n) % NZ
-        to = (2 if n == 0 else 1) if way == 0 else (6 if n == 0 else 7)
+        for piece in range(NH):
+            zs[off, piece] = out[:, piece * W:piece * W + W].astype(bf16)
+
+    def z_far(way):
+        both = pl.ds(2 * way, 2)
         return head_copy(
-            zs.at[off, half], zr.at[way, n, half], z_ss, z_rs.at[way, 2 * n + half], z_at[to]
-        )
-
-    def z_add(way, n, half):
-        off = 4 - n if way == 0 else (4 + n) % NZ
-        z_copy(way, n - 1, half).wait_recv()
-        total = zs[off, half].astype(f32) + zr[way, n - 1, half].astype(f32)
-        if n == 2 and half == way:
-            z_copy(way, 0, half).wait_recv()
-            total = total + zr[way, 0, half].astype(f32)
-        zs[off, half] = total.astype(bf16)
-        z_copy(way, n, half).start()
+            zs.at[4, both], zr.at[way, 0, both], z_ss, z_rs.at[way, 0],
+            z_at[2 if way == 0 else 6],
+        )
+
+    def z_copy(way, n, piece):
+        off = 4 - n if way == 0 else 4 + n
+        return head_copy(
+            zs.at[off, piece], zr.at[way, n, piece], z_ss, z_rs.at[way, NH * n + piece],
+            z_at[1 if way == 0 else 7],
+        )
+
+    def z_add(n, early, i):
+        for way in range(2):
+            piece = 2 * (1 - way if early else way) + i
+            off = 4 - n if way == 0 else 4 + n
+            z_copy(way, n - 1, piece).wait_recv()
+            total = zs[off, piece].astype(f32) + zr[way, n - 1, piece].astype(f32)
+            if n == 2 and not early:
+                if i == 0:
+                    z_far(way).wait_recv()
+                total = total + zr[way, 0, piece].astype(f32)
+            zs[off, piece] = total.astype(bf16)
+            z_copy(way, n, piece).start()
 
     def relay(half):
         ag_copy(half, 3, 0, sib).wait_recv()
         ag_copy(half, 3, 2, above).start()
-        sib_copy(half, 3, core).start()
         ag_copy(half, 1, 1, sib).wait_recv()
         ag_copy(half, 1, 3, below).start()
+
+    def near(half):
+        ag_copy(half, 3, 4, sib).wait_recv()
+        sib_copy(half, 3, core).start()
+        ag_copy(half, 1, 5, sib).wait_recv()
         sib_copy(half, 1, core).start()
 
     def far(half):
@@ -461,48 +483,57 @@
         gq_ref[:, hs] = (mm(g, wl[h, 0]) - rates[h] * mm(lower, kbs[h])).astype(bf16)
 
     part(3)
-    z_copy(0, 1, 1).start()
-    z_copy(0, 1, 0).start()
+    z_copy(0, 1, 2).start()
+    z_copy(0, 1, 3).start()
     part(5)
     z_copy(1, 1, 0).start()
     z_copy(1, 1, 1).start()
     part(4)
-    z_copy(0, 0, 0).start()
-    z_copy(1, 0, 1).start()
+    z_far(0).start()
+    z_far(1).start()
+    for i in range(2):
+        z_copy(0, 1, i).start()
+        z_copy(1, 1, 2 + i).start()
     part(2)
     part(6)
     relay(core)
     relay(1 - core)
-    z_add(0, 2, 1)
-    z_add(1, 2, 0)
+    near(core)
+    z_add(2, True, 0)
+    z_add(2, True, 1)
+    near(1 - core)
+    part(1)
+    part(7)
     tz_in.wait_recv()
     lax.fori_loop(0, NC * NY, turn, 0)
     far(core)
     far(1 - core)
-    z_add(0, 2, 0)
-    z_add(1, 2, 1)
-    part(1)
-    part(7)
     products(0)
+    z_add(2, False, 0)
     products(1)
-    z_add(0, 3, 1)
-    z_add(1, 3, 0)
+    z_add(2, False, 1)
+    z_add(3, True, 0)
+    z_add(3, True, 1)
+    z_add(3, False, 0)
+    z_add(3, False, 1)
     part(0)
     rs_add(0)
     rs_add(1)
-    z_add(0, 3, 0)
-    z_add(1, 3, 1)
+    leave[3].start()
     for h in range(NH):
         grad_query(h)
-
-    for half in range(2):
-        z_copy(0, 3, half).wait_recv()
-        z_copy(1, 3, half).wait_recv()
-        gt_ref[:, 2 * W * half:2 * W * (half + 1)] = (
-            zs[0, half].astype(f32) + zr[0, 3, half].astype(f32) + zr[1, 3, half].astype(f32)
+    leave[2].start()
+
+    for piece in (2, 3, 0, 1):
+        z_copy(0, 3, piece).wait_recv()
+        z_copy(1, 3, piece).wait_recv()
+        gt_ref[:, piece * W:piece * W + W] = (
+            zs[0, piece].astype(f32) + zr[0, 3, piece].astype(f32) + zr[1, 3, piece].astype(f32)
         ).astype(bf16)
+    leave[0].start()
     rs_end(0)
     rs_end(1)
+    leave[1].start()
 
     sm_sum.wait_send()
     count(ef_recv, ef_ss, ef_rs, lambda c: c.wait_send())
@@ -521,11 +552,26 @@
         seq_copy(ref, ref, rs_ss.at[half], rs_rs.at[half, 0], sib).wait_send()
     some_z = zs.at[pl.ds(0, 7)]
     head_copy(some_z, some_z, z_ss, z_rs.at[0, 0], z_at[1]).wait_send()
-
-
-def hand_over(a0, a1, a2, a3, b0, b1, b2, b3):
-    for a, b in ((a0, b0), (a1, b1), (a2, b2), (a3, b3)):
-        b[...] = a[...]
+    for copy in leave:
+        copy.wait()
+
+
+def hand_over(a0, a1, a2, a3, b0, b1, b2, b3, v0, v1, v2, v3, sems):
+    ins = [
+        pltpu.make_async_copy(a, v, sems.at[i])
+        for i, (a, v) in enumerate(((a0, v0), (a1, v1), (a2, v2), (a3, v3)))
+    ]
+    outs = [
+        pltpu.make_async_copy(v, b, sems.at[4 + i])
+        for i, (v, b) in enumerate(((v0, b0), (v1, b1), (v2, b2), (v3, b3)))
+    ]
+    for copy in ins:
+        copy.start()
+    for copy, after in zip(ins, outs):
+        copy.wait()
+        after.start()
+    for copy in outs:
+        copy.wait()
 
 
 def per_device(tokens, key_weight, queries, values, grad_out, inner_start, head_rate):
@@ -544,8 +590,9 @@
         kernel,
         out_shape=shapes,
         in_specs=[anywhere] * 6 + [smem],
-        out_specs=(vmem,) * 4,
+        out_specs=(anywhere,) * 4,
         scratch_shapes=[
+            *[pltpu.VMEM(a.shape, a.dtype) for a in shapes],
             pltpu.VMEM(tokens.shape, bf16),
             pltpu.VMEM(key_weight.shape, bf16),
             pltpu.VMEM((W, cols), bf16),
@@ -580,16 +627,17 @@
             pltpu.VMEM((2, NX, W, 2 * W), f32),
             pltpu.VMEM((2, NX, W, 2 * W), bf16),
             pltpu.VMEM((2, NX, W, 2 * W), bf16),
-            pltpu.VMEM((NZ, 2, W, 2 * W), bf16),
-            pltpu.VMEM((2, 4, 2, W, 2 * W), bf16),
+            pltpu.VMEM((NZ, NH, W, W), bf16),
+            pltpu.VMEM((2, 4, NH, W, W), bf16),
             sem((5 + KW_PARTS,)),
+            sem((4,)),
             sem, sem, sem, sem,
             sem, sem, sem, sem,
             sem((NY,)), sem((NY,)),
             sem, sem, sem, sem,
-            sem((2,)), sem((2, 4)), sem((2, 4)),
+            sem((2,)), sem((2, 6)), sem((2, 4)),
             sem((2,)), sem((2, 8)),
-            sem, sem((2, 8)),
+            sem, sem((2, 4 * NH)),
         ],
         compiler_params=pltpu.CompilerParams(
             collective_id=0, has_side_effects=True, vmem_limit_bytes=56 * 1024 * 1024
@@ -599,8 +647,9 @@
     return pl.pallas_call(
         hand_over,
         out_shape=shapes,
-        in_specs=[vmem] * 4,
-        out_specs=(vmem,) * 4,
+        in_specs=[anywhere] * 4,
+        out_specs=(anywhere,) * 4,
+        scratch_shapes=[pltpu.VMEM(a.shape, a.dtype) for a in shapes] + [sem((8,))],
         name="hand_over",
     )(*outs)
 

time: 51.1 us -> 49.4 us (0.967)
  Pallas kernels: 50.3 us -> 48.7 us
    pallas_call x1, Pallas kernels: 48.3 us -> 46.8 us  [per_device(): pl.pallas_call(kernel, out_shape=shapes, in_specs=[anywhere] * 6 + [smem]...]
where the time goes in v5:
time: 49.4 us; the launch traced here: 49.3 us
  Pallas kernels  48.7 us (99%)
  between operations  0.64 us (1%)
    pallas_call x1, Pallas kernels, per_device(): pl.pallas_call(kernel, out_shape=shapes, in_specs=[anywhere] * 6 + [smem]...  46.8 us
    pallas_call x1, Pallas kernels, per_device(): pl.pallas_call(hand_over, out_shape=shapes, in_specs=[anywhere] * 4, out_...  1.88 us

profile of v5, /device:TPU:1, one launch (start us, length us, event | category | flops | bytes accessed | tf_op | source)
XLA Modules:
  0.0 49.3 jit_solution(4478463078983940041)
XLA Ops:
  0.6 46.8 %layer.1 = (bf16[128,512]{1,0:T(8,128)(2,1)}, f32[128,512]{1,0:T(8,128)}, bf16[128,512]{1,0:T(8,128)(2,1)}, bf16[128,512]{1,0:T(8,128)(2,1)}) custom-call(bf16[128,4096]{1,0:T(8,128)(2,1)} %tok_hbm.1, bf16[4096,512]{1,0:T(8,128)(2,1)} %kw_hbm.1, bf16[128,512]{1,0:T(8,128)(2,1)} %q_hbm.1, bf16[128,512]{1,0:T(8,128)(2,1)} %v_hbm.1, bf16[128,512]{1,0:T(8,128)(2,1)} %g_hbm.1, ...), custom_call_target="tpu_custom_call" | custom-call | tf_op jit(solution)/shard_map/layer/pallas_call | solution.py:589
  47.5 1.9 %hand_over.1 = (bf16[128,512]{1,0:T(8,128)(2,1)}, f32[128,512]{1,0:T(8,128)}, bf16[128,512]{1,0:T(8,128)(2,1)}, bf16[128,512]{1,0:T(8,128)(2,1)}) custom-call(bf16[128,512]{1,0:T(8,128)(2,1)} %get-tuple-element.8.a0, f32[128,512]{1,0:T(8,128)} %get-tuple-element.9.a1, bf16[128,512]{1,0:T(8,128)(2,1)} %get-tuple-element.10.a2, ...), custom_call_target="tpu_custom_call" | custom-call | tf_op jit(solution)/shard_map/hand_over/pallas_call | solution.py:647

commit v6 on v5

--- a/solution.py
+++ b/solution.py
@@ -497,28 +497,28 @@
     part(2)
     part(6)
     relay(core)
+    near(core)
     relay(1 - core)
-    near(core)
+    near(1 - core)
+    tz_in.wait_recv()
+    lax.fori_loop(0, NC * NY, turn, 0)
     z_add(2, True, 0)
     z_add(2, True, 1)
-    near(1 - core)
+    far(core)
+    far(1 - core)
+    products(core)
+    z_add(2, False, 0)
+    products(1 - core)
+    z_add(2, False, 1)
     part(1)
     part(7)
-    tz_in.wait_recv()
-    lax.fori_loop(0, NC * NY, turn, 0)
-    far(core)
-    far(1 - core)
-    products(0)
-    z_add(2, False, 0)
-    products(1)
-    z_add(2, False, 1)
     z_add(3, True, 0)
     z_add(3, True, 1)
+    rs_add(core)
     z_add(3, False, 0)
     z_add(3, False, 1)
+    rs_add(1 - core)
     part(0)
-    rs_add(0)
-    rs_add(1)
     leave[3].start()
     for h in range(NH):
         grad_query(h)

time: 49.4 us -> 49 us (level)
  Pallas kernels: 48.7 us -> 48.2 us
where the time goes in v6:
time: 49 us; the launch traced here: 48.9 us
  Pallas kernels  48.2 us (98%)
  between operations  0.64 us (1%)
    pallas_call x1, Pallas kernels, per_device(): pl.pallas_call(kernel, out_shape=shapes, in_specs=[anywhere] * 6 + [smem]...  46.4 us
    pallas_call x1, Pallas kernels, per_device(): pl.pallas_call(hand_over, out_shape=shapes, in_specs=[anywhere] * 4, out_...  1.88 us

profile of v6, /device:TPU:1, one launch (start us, length us, event | category | flops | bytes accessed | tf_op | source)
XLA Modules:
  0.0 48.9 jit_solution(15787403426429428187)
XLA Ops:
  0.6 46.4 %layer.1 = (bf16[128,512]{1,0:T(8,128)(2,1)}, f32[128,512]{1,0:T(8,128)}, bf16[128,512]{1,0:T(8,128)(2,1)}, bf16[128,512]{1,0:T(8,128)(2,1)}) custom-call(bf16[128,4096]{1,0:T(8,128)(2,1)} %tok_hbm.1, bf16[4096,512]{1,0:T(8,128)(2,1)} %kw_hbm.1, bf16[128,512]{1,0:T(8,128)(2,1)} %q_hbm.1, bf16[128,512]{1,0:T(8,128)(2,1)} %v_hbm.1, bf16[128,512]{1,0:T(8,128)(2,1)} %g_hbm.1, ...), custom_call_target="tpu_custom_call" | custom-call | tf_op jit(solution)/shard_map/layer/pallas_call | solution.py:589
  47.0 1.9 %hand_over.1 = (bf16[128,512]{1,0:T(8,128)(2,1)}, f32[128,512]{1,0:T(8,128)}, bf16[128,512]{1,0:T(8,128)(2,1)}, bf16[128,512]{1,0:T(8,128)(2,1)}) custom-call(bf16[128,512]{1,0:T(8,128)(2,1)} %get-tuple-element.8.a0, f32[128,512]{1,0:T(8,128)} %get-tuple-element.9.a1, bf16[128,512]{1,0:T(8,128)(2,1)} %get-tuple-element.10.a2, ...), custom_call_target="tpu_custom_call" | custom-call | tf_op jit(solution)/shard_map/hand_over/pallas_call | solution.py:647

commit v7 on v6

--- a/solution.py
+++ b/solution.py
@@ -494,10 +494,10 @@
     for i in range(2):
         z_copy(0, 1, i).start()
         z_copy(1, 1, 2 + i).start()
+    relay(core)
+    near(core)
     part(2)
     part(6)
-    relay(core)
-    near(core)
     relay(1 - core)
     near(1 - core)
     tz_in.wait_recv()

time: 49 us -> 49.7 us (1.014)
  Pallas kernels: 48.2 us -> 48.9 us
    pallas_call x1, Pallas kernels: 46.4 us -> 47.1 us  [per_device(): pl.pallas_call(kernel, out_shape=shapes, in_specs=[anywhere] * 6 + [smem]...]
where the time goes in v7:
time: 49.7 us; the launch traced here: 49.6 us
  Pallas kernels  48.9 us (98%)
  between operations  0.64 us (1%)
    pallas_call x1, Pallas kernels, per_device(): pl.pallas_call(kernel, out_shape=shapes, in_specs=[anywhere] * 6 + [smem]...  47.1 us
    pallas_call x1, Pallas kernels, per_device(): pl.pallas_call(hand_over, out_shape=shapes, in_specs=[anywhere] * 4, out_...  1.88 us

profile of v7, /device:TPU:1, one launch (start us, length us, event | category | flops | bytes accessed | tf_op | source)
XLA Modules:
  0.0 49.6 jit_solution(2092779831258396330)
XLA Ops:
  0.6 47.1 %layer.1 = (bf16[128,512]{1,0:T(8,128)(2,1)}, f32[128,512]{1,0:T(8,128)}, bf16[128,512]{1,0:T(8,128)(2,1)}, bf16[128,512]{1,0:T(8,128)(2,1)}) custom-call(bf16[128,4096]{1,0:T(8,128)(2,1)} %tok_hbm.1, bf16[4096,512]{1,0:T(8,128)(2,1)} %kw_hbm.1, bf16[128,512]{1,0:T(8,128)(2,1)} %q_hbm.1, bf16[128,512]{1,0:T(8,128)(2,1)} %v_hbm.1, bf16[128,512]{1,0:T(8,128)(2,1)} %g_hbm.1, ...), custom_call_target="tpu_custom_call" | custom-call | tf_op jit(solution)/shard_map/layer/pallas_call | solution.py:589
  47.7 1.9 %hand_over.1 = (bf16[128,512]{1,0:T(8,128)(2,1)}, f32[128,512]{1,0:T(8,128)}, bf16[128,512]{1,0:T(8,128)(2,1)}, bf16[128,512]{1,0:T(8,128)(2,1)}) custom-call(bf16[128,512]{1,0:T(8,128)(2,1)} %get-tuple-element.8.a0, f32[128,512]{1,0:T(8,128)} %get-tuple-element.9.a1, bf16[128,512]{1,0:T(8,128)(2,1)} %get-tuple-element.10.a2, ...), custom_call_target="tpu_custom_call" | custom-call | tf_op jit(solution)/shard_map/hand_over/pallas_call | solution.py:647
